TPU v7x, 256 devices: a whole 4x4x8 slice. The times are simulated.
256 devices in a mesh: pair: 64 (over z, y, core), rep: 4 (over x).
Axes of the slice: x: 4, y: 4, z: 8, core: 2. Of those that a mesh axis runs over, the one named last changes fastest.
Arguments:
- amplitudes: float32 [4096, 32768], P('pair'), may hold values from -6 to 6
- integrals: float32 [32768, 1536], P(('pair', 'rep')), may hold values from -0.375 to 0.375
- row_irrep: int32 [4096], replicated, may hold values from 0 to 7, as said below
- pair_irrep: int32 [32768], P(('pair', 'rep')), may hold values from 0 to 7, as said below
- slab_irrep: int32 [1536], replicated, may hold values from 0 to 7, as said below
Outputs:
- ladder: float32 [4096, 1536], P('pair', 'rep')
Inputs may be any that keep to these rules, and one draw needn't show every extreme that they name: `row_irrep`: irrep labels are non-decreasing within each aligned block of 64 occupied pairs: contiguous symmetry blocks of varying size. `pair_irrep`: irrep labels are non-decreasing within each aligned block of 128 virtual pairs: contiguous symmetry blocks of varying size. `slab_irrep`: irrep labels are non-decreasing within each aligned block of 1536 // 4 slab pairs: contiguous symmetry blocks of varying size.
All inputs are finite; a program needn't handle non-finite values.
Results may differ from a plain program's by a relative error of at most 0.0003.
Values sent between devices are 32-bit elements; how exact they have to be, the bound alone decides.
No kernel may reach another device: no remote copies, remote signals or barrier semaphores. Data moves between devices by JAX's collectives and lax.ppermute only.
A program may use at most 128 MiB of HBM per device.

v0:
```python
import jax
import jax.numpy as jnp
from jax import lax
from jax.sharding import PartitionSpec as P


def per_device(amplitudes, integrals, row_irrep, pair_irrep, slab_irrep):
    pair_count = lax.axis_size("pair")
    rep_count = lax.axis_size("rep")
    rep_index = lax.axis_index("rep")
    row_count = amplitudes.shape[0]
    columns = integrals.shape[0]
    kept_slab = jnp.where(
        pair_irrep[:, None] == slab_irrep[None, :], integrals, jnp.zeros_like(integrals)
    )
    grouped = amplitudes.reshape(row_count, pair_count, rep_count, columns)
    selected = lax.dynamic_index_in_dim(grouped, rep_index, 2, keepdims=False)
    arrived = lax.all_to_all(selected, "pair", split_axis=1, concat_axis=0, tiled=True)
    arrived = arrived.reshape(pair_count * row_count, columns)
    kept_rows = jnp.where(
        row_irrep[:, None] == pair_irrep[None, :], arrived, jnp.zeros_like(arrived)
    )
    partial_value = jnp.dot(
        kept_rows, kept_slab, precision=lax.Precision.HIGHEST, preferred_element_type=jnp.float32
    )
    reduced = lax.psum_scatter(partial_value, "rep", scatter_dimension=1, tiled=True)
    return lax.psum_scatter(reduced, "pair", scatter_dimension=0, tiled=True)


def solution(mesh):
    placed = (P("pair", None), P(("pair", "rep"), None), P(), P(("pair", "rep")), P())
    return jax.shard_map(
        per_device, mesh=mesh, in_specs=placed, out_specs=P("pair", "rep"), check_vma=False
    )
```

profile of v0, /device:TPU:2, one launch (start us, length us, event | category | flops | bytes accessed | tf_op | source)
XLA Modules:
  0.0 486.5 jit_solution(16756714096367985581)
XLA Ops:
  6.5 0.0 reduce-scatter.3.cloned.1.call-start
  6.5 10.8 %reshape.11 = f32[64,64,4,128]{3,2,1,0:T(4,128)} reshape(f32[64,32768]{1,0:T(8,128)} %param.5) | data formatting | bytes 16777216 | tf_op jit(solution)/shard_map/reshape | solution.py:16
  17.4 5.6 %constant_dynamic-slice_fusion = f32[64,64,1,128]{3,2,1,0:T(1,128)S(1)} fusion(f32[64,64,4,128]{3,2,1,0:T(4,128)} %reshape.11, s32[]{:T(128)S(6)} %select_n.12), kind=kLoop, calls=%fused_computation.8 | loop fusion | bytes 4194308 | tf_op jit(solution)/shard_map/jit(dynamic_index_in_dim)/dynamic_slice | solution.py:17
  23.0 1.2 copy.9
  24.3 0.0 copy-start.1
  24.3 0.0 copy-start.3
  24.3 63.3 %all_to_all.15 = f32[64,64,128]{2,0,1:T(8,128)S(1)} all-to-all(f32[64,64,128]{2,0,1:T(8,128)S(1)} %bitcast.10), channel_id=1, replica_groups=mesh['pair'=64,'rep'=4] {'pair'}, dimensions={1} | all-to-all | bytes 4194304 | tf_op jit(solution)/shard_map/all_to_all | solution.py:18
  87.5 0.0 copy-done.1
  87.5 0.0 copy-done.3
  87.5 0.0 copy-start
  87.5 0.0 copy-start.2
  87.6 1.9 bitcast_select_fusion
  89.4 0.0 copy-done
  89.4 0.0 copy-done.2
  89.5 23.2 %fusion = f32[4096,1536]{1,0:T(8,128)} fusion(f32[4096,128]{1,0:T(8,128)S(1)} %bitcast_select_fusion, f32[128,1536]{1,0:T(8,128)S(1)} %copy-done, s32[1536]{0:T(1024)S(1)} %copy-done.2, s32[128]{0:T(128)S(1)} %copy-done.3), kind=kOutput, calls=%fused_computation.2 | convolution fusion | flops 9664069632 | bytes 28056064 | tf_op jit(solution)/shard_map/dot_general | solution.py:23
  112.7 0.0 reduce-scatter.3.cloned.1.call-update
  112.7 0.0 reduce-scatter.5.cloned.1.call-start
  112.8 213.2 %reduce-scatter.3.cloned.1.call-done = f32[4096,384]{1,0:T(8,128)} async-done(((f32[4096,1536]{1,0:T(8,128)}), f32[4096,384]{1,0:T(8,128)}) %reduce-scatter.3.cloned.1.call-update) | async-done | bytes 6291472 | tf_op jit(solution)/shard_map/reduce_scatter | solution.py:26
  326.0 0.0 reduce-scatter.5.cloned.1.call-update
  326.0 153.7 %reduce-scatter.5.cloned.1.call-done = f32[64,384]{1,0:T(8,128)} async-done(((f32[4096,384]{1,0:T(8,128)}), f32[64,384]{1,0:T(8,128)}) %reduce-scatter.5.cloned.1.call-update) | async-done | bytes 98320 | tf_op jit(solution)/shard_map/reduce_scatter | solution.py:27
Async XLA Ops:
  6.5 319.4 %reduce-scatter.3.cloned.1.call-start = ((), (), s32[]{:S(2)}) async-start(), calls=%async_computation.3 | async-start | bytes 31457280 | tf_op jit(solution)/shard_map/reduce_scatter | solution.py:26
  24.3 63.3 %copy-start.1 = (s32[4096]{0:T(1024)S(1)}, s32[4096]{0:T(1024)}, u32[]{:S(2)}) copy-start(s32[4096]{0:T(1024)} %param.7) | copy-start | bytes 49156
  24.3 63.3 %copy-start.3 = (s32[128]{0:T(128)S(1)}, s32[128]{0:T(128)}, u32[]{:S(2)}) copy-start(s32[128]{0:T(128)} %param.8) | copy-start | bytes 1540
  87.5 1.9 copy-start
  87.5 1.9 copy-start.2
  112.7 367.0 %reduce-scatter.5.cloned.1.call-start = ((), (), s32[]{:S(2)}) async-start(), calls=%async_computation.4 | async-start | bytes 6389760 | tf_op jit(solution)/shard_map/reduce_scatter | solution.py:27
Sparse Core Ops, SparseCore 0:
  112.8 213.0 reduce-scatter.2
  330.7 148.9 reduce-scatter.4
where the time goes:
time: 487 us
  waiting for transfers between devices  367 us (75%)
  blocking collectives  63.3 us (13%)
  matrix products  23.2 us (5%)
  local copies, waits for them, and re-layouts  17.7 us (4%)
  between operations  13.5 us (3%)
    reduce_scatter x1, waiting for transfers between devices, per_device(): lax.psum_scatter(partial_value, 'rep', scatter_dimension=1, tiled=True)  213 us
    reduce_scatter x1, waiting for transfers between devices, per_device(): return lax.psum_scatter(reduced, 'pair', scatter_dimension=0, tiled=True)  154 us
    all_to_all x1, blocking collectives, per_device(): lax.all_to_all(selected, 'pair', split_axis=1, concat_axis=0, tiled=True)  63.3 us
    dot_general x1, matrix products, per_device(): jnp.dot(kept_rows, kept_slab, precision=lax.Precision.HIGHEST, preferred_...  23.2 us
    reshape x1, local copies, waits for them, and re-layouts, per_device(): grouped = amplitudes.reshape(row_count, pair_count, rep_count, columns)  10.8 us
  transfers between devices with their start and end apart: 2, of which 2 were waited for; matrix products, arithmetic and copies ran while one was open for 0% of the time, Pallas kernels for 0%

commit v1 on v0

v1 whole, which is shorter than its diff:
```python
import functools

import jax
import jax.numpy as jnp
from jax import lax
from jax.experimental import pallas as pl
from jax.experimental.pallas import tpu as pltpu
from jax.sharding import Mesh
from jax.sharding import PartitionSpec as P

Z, Y, C, X = 8, 4, 2, 4
IRREPS = 8
ROW_DEV = 64
AB_DEV = 128
CD = 1536
CD_DEV = CD // X
WIDTH = 240
SLOTS = WIDTH - 1
BLOCKS = Z * C
AB_GROUP = BLOCKS * AB_DEV
SHIFTS = (1, Y - 1, 2)
VMEM = pl.BlockSpec(memory_space=pltpu.VMEM)
SMEM = pl.BlockSpec(memory_space=pltpu.SMEM)
ANY = pl.BlockSpec(memory_space=pl.ANY)
PARAMS = pltpu.CompilerParams(vmem_limit_bytes=40 * 2**20)
NT = (((1,), (1,)), ((), ()))
NN = (((1,), (0,)), ((), ()))


def split(value):
    high = value.astype(jnp.bfloat16)
    low = (value - high.astype(jnp.float32)).astype(jnp.bfloat16)
    return high, low


def one_hot(rank, offset):
    slot = lax.broadcasted_iota(jnp.int32, (WIDTH, rank.shape[1]), 0)
    hit = (slot == rank - offset) & (slot < SLOTS)
    return jnp.where(hit, 1.0, 0.0).astype(jnp.bfloat16)


def label_column(row):
    return jnp.broadcast_to(row, (128, 128)).T


def rank_kernel(slab_ref, rank_ref, rounds_ref):
    slab = slab_ref[...]
    mine = slab == lax.broadcasted_iota(jnp.int32, (IRREPS, CD), 0)
    lane = lax.broadcasted_iota(jnp.int32, (IRREPS, CD), 1)
    count = mine.astype(jnp.int32)
    shift = 1
    while shift < CD:
        count = count + jnp.where(lane >= shift, pltpu.roll(count, shift, 1), 0)
        shift *= 2
    rank_ref[...] = jnp.sum(jnp.where(mine, count, 0), axis=0, keepdims=True) - 1
    rounds_ref[0] = lax.div(jnp.max(count) + (SLOTS - 1), SLOTS)


def compact_kernel(round_ref, integrals_ref, pair_ref, slab_ref, rank_ref, out_ref):
    labels = label_column(pair_ref[...].astype(jnp.float32))
    slab = slab_ref[...].astype(jnp.float32)
    kept = jnp.concatenate(
        [
            jnp.where(labels == slab[:, at : at + 128], integrals_ref[:, at : at + 128], 0.0)
            for at in range(0, CD, 128)
        ],
        axis=1,
    )
    high, low = split(kept)
    chosen = one_hot(rank_ref[...], round_ref[0] * SLOTS)
    packed = lax.dot_general(chosen, high, NT, preferred_element_type=jnp.float32)
    packed += lax.dot_general(chosen, low, NT, preferred_element_type=jnp.float32)
    slot = lax.broadcasted_iota(jnp.int32, (WIDTH, AB_DEV), 0)
    out_ref[...] = jnp.where(slot == SLOTS, pair_ref[...].astype(jnp.float32), packed)


def select_kernel(at_ref, amplitudes_ref, *refs):
    outs, sems = refs[:-1], refs[-1]
    y, x = at_ref[1], at_ref[3]
    copies = []
    for d, shift in enumerate(SHIFTS):
        target = lax.rem(y + shift, Y)
        for block in range(BLOCKS):
            z, c = divmod(block, C)
            source = pl.multiple_of((((z * Y + target) * C + c) * X + x) * AB_DEV, AB_DEV)
            copy = pltpu.make_async_copy(
                amplitudes_ref.at[:, pl.ds(source, AB_DEV)],
                outs[d].at[:, pl.ds(block * AB_DEV, AB_DEV)],
                sems.at[d, block],
            )
            copy.start()
            copies.append(copy)
    for copy in copies:
        copy.wait()


def product_kernel(at_ref, amplitudes_ref, *refs):
    arrived = refs[:3]
    blocks = refs[3 : 3 + BLOCKS]
    rows_ref = refs[3 + BLOCKS]
    outs = refs[4 + BLOCKS : 8 + BLOCKS]
    own, thigh, tlow, vhigh, vlow, sems = refs[8 + BLOCKS :]
    z, y, c, x = at_ref[0], at_ref[1], at_ref[2], at_ref[3]
    copies = []
    for block in range(BLOCKS):
        bz, bc = divmod(block, C)
        source = pl.multiple_of((((bz * Y + y) * C + bc) * X + x) * AB_DEV, AB_DEV)
        copy = pltpu.make_async_copy(
            amplitudes_ref.at[:, pl.ds(source, AB_DEV)],
            own.at[:, pl.ds(block * AB_DEV, AB_DEV)],
            sems.at[block],
        )
        copy.start()
        copies.append(copy)
    columns = []
    for k, block in enumerate(blocks):
        value = block[...]
        at = pl.ds(k * AB_DEV, AB_DEV)
        high, low = split(value)
        vhigh[:, at] = high
        vlow[:, at] = low
        columns.append(value[SLOTS : SLOTS + 1, :])
    for copy in copies:
        copy.wait()
    for d, (ref, shift) in enumerate(zip((own,) + tuple(arrived), (0,) + SHIFTS)):
        source = lax.rem(y - shift + Y, Y)
        both = label_column(rows_ref[pl.ds(z * Y + source, 1), :].astype(jnp.float32))
        labels = jnp.where(c == 0, both[:ROW_DEV], both[ROW_DEV:])
        for k in range(BLOCKS):
            steps, other = divmod(k, C)
            bz = lax.rem(z + steps, Z)
            bc = lax.rem(c + other, C)
            at = pl.ds(pl.multiple_of((bz * C + bc) * AB_DEV, AB_DEV), AB_DEV)
            kept = jnp.where(labels == columns[k], ref[:, at], 0.0)
            high, low = split(kept)
            thigh[d * ROW_DEV : (d + 1) * ROW_DEV, k * AB_DEV : (k + 1) * AB_DEV] = high
            tlow[d * ROW_DEV : (d + 1) * ROW_DEV, k * AB_DEV : (k + 1) * AB_DEV] = low
    total = lax.dot_general(thigh[...], vhigh[...], NT, preferred_element_type=jnp.float32)
    total += lax.dot_general(thigh[...], vlow[...], NT, preferred_element_type=jnp.float32)
    total += lax.dot_general(tlow[...], vhigh[...], NT, preferred_element_type=jnp.float32)
    for d, out in enumerate(outs):
        out[...] = total[d * ROW_DEV : (d + 1) * ROW_DEV]


def sum_kernel(a_ref, b_ref, c_ref, d_ref, out_ref):
    out_ref[...] = (a_ref[...] + b_ref[...]) + (c_ref[...] + d_ref[...])


def expand_kernel(round_ref, at_ref, a_ref, b_ref, c_ref, d_ref, rows_ref, slab_ref, rank_ref, out_ref):
    z, y, c, x = at_ref[0], at_ref[1], at_ref[2], at_ref[3]
    total = (a_ref[...] + b_ref[...]) + (c_ref[...] + d_ref[...])
    at = pl.ds(pl.multiple_of(x * CD_DEV, CD_DEV), CD_DEV)
    chosen = one_hot(rank_ref[:, at], round_ref[0] * SLOTS)
    high = total.astype(jnp.bfloat16)
    rest = total - high.astype(jnp.float32)
    middle, low = split(rest)
    wide = lax.dot_general(high, chosen, NN, preferred_element_type=jnp.float32)
    wide += lax.dot_general(middle, chosen, NN, preferred_element_type=jnp.float32)
    wide += lax.dot_general(low, chosen, NN, preferred_element_type=jnp.float32)
    both = label_column(rows_ref[pl.ds(z * Y + y, 1), :].astype(jnp.float32))
    labels = jnp.where(c == 0, both[:ROW_DEV], both[ROW_DEV:])
    slab = slab_ref[:, at].astype(jnp.float32)
    for k in range(0, CD_DEV, 128):
        out_ref[:, k : k + 128] = jnp.where(labels == slab[:, k : k + 128], wide[:, k : k + 128], 0.0)


def shifted(value, axis, by):
    size = {"z": Z, "y": Y, "c": C, "x": X}[axis]
    return lax.ppermute(value, axis, [(i, (i + by) % size) for i in range(size)])


def f32(*shape):
    return jax.ShapeDtypeStruct(shape, jnp.float32)


def per_device(amplitudes, integrals, row_irrep, pair_irrep, slab_irrep):
    at = jnp.stack([lax.axis_index(a) for a in ("z", "y", "c", "x")]).astype(jnp.int32)
    rows = row_irrep.reshape(-1, 128)
    pair = pair_irrep.reshape(1, AB_DEV)
    slab = slab_irrep.reshape(1, CD)
    rank, rounds = pl.pallas_call(
        rank_kernel,
        out_shape=(jax.ShapeDtypeStruct((1, CD), jnp.int32), jax.ShapeDtypeStruct((1,), jnp.int32)),
        in_specs=[VMEM],
        out_specs=(VMEM, SMEM),
        name="rank",
    )(slab)

    pieces = pl.pallas_call(
        select_kernel,
        out_shape=[f32(ROW_DEV, AB_GROUP)] * 3,
        in_specs=[SMEM, ANY],
        out_specs=[ANY] * 3,
        scratch_shapes=[pltpu.SemaphoreType.DMA((3, BLOCKS))],
        name="select",
    )(at, amplitudes)
    arrived = [shifted(piece, "y", shift) for piece, shift in zip(pieces, SHIFTS)]

    def ladder_round(number):
        number = number.reshape(1)
        packed = pl.pallas_call(
            compact_kernel,
            out_shape=f32(WIDTH, AB_DEV),
            in_specs=[SMEM, VMEM, VMEM, VMEM, VMEM],
            out_specs=VMEM,
            compiler_params=PARAMS,
            name="compact",
        )(number, integrals, pair, slab, rank)
        blocks = {0: packed}
        up = down = packed
        for step in range(1, Z // 2 + 1):
            up = shifted(up, "z", -1)
            blocks[step] = up
            if step < Z // 2:
                down = shifted(down, "z", 1)
                blocks[Z - step] = down
        gathered = []
        for step in range(Z):
            gathered += [blocks[step], shifted(blocks[step], "c", 1)]
        parts = pl.pallas_call(
            product_kernel,
            out_shape=[f32(ROW_DEV, WIDTH)] * 4,
            in_specs=[SMEM, ANY] + [VMEM] * (4 + BLOCKS),
            out_specs=[VMEM] * 4,
            scratch_shapes=[
                pltpu.VMEM((ROW_DEV, AB_GROUP), jnp.float32),
                pltpu.VMEM((Y * ROW_DEV, AB_GROUP), jnp.bfloat16),
                pltpu.VMEM((Y * ROW_DEV, AB_GROUP), jnp.bfloat16),
                pltpu.VMEM((WIDTH, AB_GROUP), jnp.bfloat16),
                pltpu.VMEM((WIDTH, AB_GROUP), jnp.bfloat16),
                pltpu.SemaphoreType.DMA((BLOCKS,)),
            ],
            compiler_params=PARAMS,
            name="product",
        )(at, amplitudes, *arrived, *gathered, rows)
        back = [shifted(part, "y", -shift) for part, shift in zip(parts[1:], SHIFTS)]
        mine = pl.pallas_call(
            sum_kernel,
            out_shape=f32(ROW_DEV, WIDTH),
            in_specs=[VMEM] * 4,
            out_specs=VMEM,
            name="sum",
        )(parts[0], *back)
        others = [shifted(mine, "x", shift) for shift in (1, X - 1, 2)]
        return pl.pallas_call(
            expand_kernel,
            out_shape=f32(ROW_DEV, CD_DEV),
            in_specs=[SMEM, SMEM] + [VMEM] * 7,
            out_specs=VMEM,
            compiler_params=PARAMS,
            name="expand",
        )(number, at, mine, *others, rows, slab, rank)

    first = ladder_round(jnp.zeros((), jnp.int32))
    _, ladder = lax.while_loop(
        lambda state: state[0] < rounds[0],
        lambda state: (state[0] + 1, state[1] + ladder_round(state[0])),
        (jnp.ones((), jnp.int32), first),
    )
    return ladder


def solution(mesh):
    grid = Mesh(mesh.devices.reshape(Z, Y, C, X), ("z", "y", "c", "x"))
    placed = (P(("z", "y", "c"), None), P(("z", "y", "c", "x"), None), P(), P(("z", "y", "c", "x")), P())
    return jax.shard_map(
        per_device, mesh=grid, in_specs=placed, out_specs=P(("z", "y", "c"), "x"), check_vma=False
    )
```

time: 487 us -> 120 us (0.25)
  waiting for transfers between devices: 367 us -> 28.5 us
  blocking collectives: 63.3 us -> 0 us
  Pallas kernels: 0 us -> 58.1 us
  starting transfers between devices: 0.04 us -> 28.2 us
  matrix products: 23.2 us -> 0 us
  local copies, waits for them, and re-layouts: 17.7 us -> 3.47 us
  between operations: 13.5 us -> 0.13 us
    reduce_scatter x2 -> x0, waiting for transfers between devices: 367 us -> none  [the longest x1 213 us: per_device(): lax.psum_scatter(partial_value, 'rep', scatter_dimension=1, tiled=True)]
    all_to_all x1 -> x0, blocking collectives: 63.3 us -> none  [per_device(): lax.all_to_all(selected, 'pair', split_axis=1, concat_axis=0, tiled=True)]
    pallas_call x0 -> x6, Pallas kernels: none -> 58.1 us  [the longest x1 49.7 us: per_device(): pl.pallas_call(select_kernel, out_shape=[f32(ROW_DEV, AB_GROUP)] * 3, in_...]
    ppermute x0 -> x24, waiting for transfers between devices: none -> 28.5 us  [shifted(): lax.ppermute(value, axis, [(i, (i + by) % size) for i in range(size)])]
    ppermute x0 -> x24, starting transfers between devices: none -> 28.2 us  [shifted(): lax.ppermute(value, axis, [(i, (i + by) % size) for i in range(size)])]
    dot_general x1 -> x0, matrix products: 23.2 us -> none  [per_device(): jnp.dot(kept_rows, kept_slab, precision=lax.Precision.HIGHEST, preferred_...]
    reshape x1, local copies, waits for them, and re-layouts: 10.8 us -> 0.71 us  [per_device(): slab = slab_irrep.reshape(1, CD)]
    dynamic_slice x1 -> x0, local copies, waits for them, and re-layouts: 5.65 us -> none  [per_device(): selected = lax.dynamic_index_in_dim(grouped, rep_index, 2, keepdims=False)]
  transfers between devices with their start and end apart: 2 -> 24, of which waited for: 2 -> 12; matrix products, arithmetic and copies ran while one was open for 0% -> 0% of each run, Pallas kernels for 0% -> 42%
where the time goes in v1:
time: 120 us; the launch traced here: 119 us
  Pallas kernels  58.1 us (48%)
  waiting for transfers between devices  28.5 us (24%)
  starting transfers between devices  28.2 us (24%)
  local copies, waits for them, and re-layouts  3.47 us (3%)
    pallas_call x1, Pallas kernels, per_device(): pl.pallas_call(select_kernel, out_shape=[f32(ROW_DEV, AB_GROUP)] * 3, in_...  49.7 us
    ppermute x24, waiting for transfers between devices, shifted(): lax.ppermute(value, axis, [(i, (i + by) % size) for i in range(size)])  28.5 us
    ppermute x24, starting transfers between devices, shifted(): lax.ppermute(value, axis, [(i, (i + by) % size) for i in range(size)])  28.2 us
    pallas_call x1, Pallas kernels, ladder_round(): pl.pallas_call(product_kernel, out_shape=[f32(ROW_DEV, WIDTH)] * 4, in_sp...  2.98 us
    unnamed x18, local copies, waits for them, and re-layouts  2.75 us
  transfers between devices with their start and end apart: 24, of which 12 were waited for; matrix products, arithmetic and copies ran while one was open for 0% of the time, Pallas kernels for 42%

profile of v1, /device:TPU:2, one launch (start us, length us, event | category | flops | bytes accessed | tf_op | source)
XLA Modules:
  0.0 119.1 jit_solution(12730390962265036044)
XLA Ops:
  0.0 0.7 reshape.13.slab_ref
  0.7 1.3 %rank.1 = (s32[1,1536]{1,0:T(1,128)S(1)}, s32[1]{0:T(128)}) custom-call(s32[1,1536]{1,0:T(1,128)S(1)} %reshape.13.slab_ref), custom_call_target="tpu_custom_call" | custom-call | tf_op jit(solution)/shard_map/rank/pallas_call | solution.py:181
  2.0 1.7 %compact.2.refs_3_ = f32[240,128]{1,0:T(8,128)S(1)} custom-call(s32[1]{0:T(128)} %constant.17.clone.1.round_ref, f32[128,1536]{1,0:T(8,128)} %integrals_ref.1, s32[1,128]{1,0:T(1,128)} %bitcast.14, s32[1,1536]{1,0:T(1,128)S(1)} %reshape.13.slab_ref, s32[1,1536]{1,0:T(1,128)S(1)} %get-tuple-element.216.rank_ref), custom_call_target="tpu_custom_call" | custom-call | tf_op jit(solution)/shard_map/compact/pallas_call | solution.py:201
  3.7 5.9 %collective-permute-start.25 = (f32[240,128]{1,0:T(8,128)S(1)}, f32[240,128]{1,0:T(8,128)S(1)}, u32[]{:S(2)}, u32[]{:S(2)}) collective-permute-start(f32[240,128]{1,0:T(8,128)S(1)} %compact.2.refs_3_), channel_id=1, source_target_pairs={{0,224},{32,0},{64,32},{96,64},{128,96},{160,128},{192,160},{224,1... | collective-permute-start | bytes 368648 | tf_op jit(solution)/shard_map/ppermute | solution.py:169
  9.7 2.6 %collective-permute-done.25.refs_5_ = f32[240,128]{1,0:T(8,128)S(1)} collective-permute-done((f32[240,128]{1,0:T(8,128)S(1)}, f32[240,128]{1,0:T(8,128)S(1)}, u32[]{:S(2)}, u32[]{:S(2)}) %collective-permute-start.25) | collective-permute-done | bytes 122912 | tf_op jit(solution)/shard_map/ppermute | solution.py:169
  12.3 3.7 %collective-permute-start.27 = (f32[240,128]{1,0:T(8,128)S(1)}, f32[240,128]{1,0:T(8,128)S(1)}, u32[]{:S(2)}, u32[]{:S(2)}) collective-permute-start(f32[240,128]{1,0:T(8,128)S(1)} %collective-permute-done.25.refs_5_), channel_id=1, source_target_pairs={{0,224},{32,0},{64,32},{96,64},{128,96},{160,128},{192,160},{224,1... | collective-permute-start | bytes 368648 | tf_op jit(solution)/shard_map/ppermute | solution.py:169
  16.5 49.7 %select.1 = (f32[64,2048]{1,0:T(8,128)}, f32[64,2048]{1,0:T(8,128)}, f32[64,2048]{1,0:T(8,128)}) custom-call(s32[4]{0:T(128)S(1)} %pad_add_fusion.at_ref, f32[64,32768]{1,0:T(8,128)} %amplitudes_ref.3), custom_call_target="tpu_custom_call" | custom-call | tf_op jit(solution)/shard_map/select/pallas_call | solution.py:189
  66.3 1.7 %collective-permute-start.21 = (f32[64,2048]{1,0:T(8,128)}, f32[64,2048]{1,0:T(8,128)S(1)}, u32[]{:S(2)}, u32[]{:S(2)}) collective-permute-start(f32[64,2048]{1,0:T(8,128)} %get-tuple-element.86), channel_id=1, source_target_pairs={{0,8},{8,16},{16,24},{24,0},{1,9},{9,17},{17,25},{25,1},{2,10},{10... | collective-permute-start | bytes 1572872 | tf_op jit(solution)/shard_map/ppermute | solution.py:169
  68.0 1.7 %collective-permute-start.22 = (f32[64,2048]{1,0:T(8,128)}, f32[64,2048]{1,0:T(8,128)S(1)}, u32[]{:S(2)}, u32[]{:S(2)}) collective-permute-start(f32[64,2048]{1,0:T(8,128)} %get-tuple-element.87), channel_id=1, source_target_pairs={{0,24},{8,0},{16,8},{24,16},{1,25},{9,1},{17,9},{25,17},{2,26},{10... | collective-permute-start | bytes 1572872 | tf_op jit(solution)/shard_map/ppermute | solution.py:169
  69.6 2.0 %collective-permute-start.23 = (f32[64,2048]{1,0:T(8,128)}, f32[64,2048]{1,0:T(8,128)S(1)}, u32[]{:S(2)}, u32[]{:S(2)}) collective-permute-start(f32[64,2048]{1,0:T(8,128)} %get-tuple-element.88), channel_id=1, source_target_pairs={{0,16},{8,24},{16,0},{24,8},{1,17},{9,25},{17,1},{25,9},{2,18},{10... | collective-permute-start | bytes 1572872 | tf_op jit(solution)/shard_map/ppermute | solution.py:169
  71.6 3.2 %collective-permute-start.29 = (f32[240,128]{1,0:T(8,128)S(1)}, f32[240,128]{1,0:T(8,128)S(1)}, u32[]{:S(2)}, u32[]{:S(2)}) collective-permute-start(f32[240,128]{1,0:T(8,128)S(1)} %collective-permute-done.27.refs_7_), channel_id=1, source_target_pairs={{0,224},{32,0},{64,32},{96,64},{128,96},{160,128},{192,160},{224,1... | collective-permute-start | bytes 368648 | tf_op jit(solution)/shard_map/ppermute | solution.py:169
  74.9 2.4 %collective-permute-done.29.refs_9_ = f32[240,128]{1,0:T(8,128)S(1)} collective-permute-done((f32[240,128]{1,0:T(8,128)S(1)}, f32[240,128]{1,0:T(8,128)S(1)}, u32[]{:S(2)}, u32[]{:S(2)}) %collective-permute-start.29) | collective-permute-done | bytes 122912 | tf_op jit(solution)/shard_map/ppermute | solution.py:169
  77.3 3.6 %collective-permute-done.35.refs_13_ = f32[240,128]{1,0:T(8,128)S(1)} collective-permute-done((f32[240,128]{1,0:T(8,128)S(1)}, f32[240,128]{1,0:T(8,128)S(1)}, u32[]{:S(2)}, u32[]{:S(2)}) %collective-permute-start.35) | collective-permute-done | bytes 122912 | tf_op jit(solution)/shard_map/ppermute | solution.py:169
  81.0 1.3 %collective-permute-start.31 = (f32[240,128]{1,0:T(8,128)S(1)}, f32[240,128]{1,0:T(8,128)S(1)}, u32[]{:S(2)}, u32[]{:S(2)}) collective-permute-start(f32[240,128]{1,0:T(8,128)S(1)} %collective-permute-done.29.refs_9_), channel_id=1, source_target_pairs={{0,224},{32,0},{64,32},{96,64},{128,96},{160,128},{192,160},{224,1... | collective-permute-start | bytes 368648 | tf_op jit(solution)/shard_map/ppermute | solution.py:169
  82.4 4.3 %collective-permute-done.31.refs_11_ = f32[240,128]{1,0:T(8,128)S(1)} collective-permute-done((f32[240,128]{1,0:T(8,128)S(1)}, f32[240,128]{1,0:T(8,128)S(1)}, u32[]{:S(2)}, u32[]{:S(2)}) %collective-permute-start.31) | collective-permute-done | bytes 122912 | tf_op jit(solution)/shard_map/ppermute | solution.py:169
  87.2 0.8 collective-permute-done.36.refs_14_
  88.0 4.5 %collective-permute-done.22.refs_1_ = f32[64,2048]{1,0:T(8,128)S(1)} collective-permute-done((f32[64,2048]{1,0:T(8,128)}, f32[64,2048]{1,0:T(8,128)S(1)}, u32[]{:S(2)}, u32[]{:S(2)}) %collective-permute-start.22) | collective-permute-done | bytes 524320 | tf_op jit(solution)/shard_map/ppermute | solution.py:169
  92.5 1.7 %collective-permute-done.23.refs_2_ = f32[64,2048]{1,0:T(8,128)S(1)} collective-permute-done((f32[64,2048]{1,0:T(8,128)}, f32[64,2048]{1,0:T(8,128)S(1)}, u32[]{:S(2)}, u32[]{:S(2)}) %collective-permute-start.23) | collective-permute-done | bytes 524320 | tf_op jit(solution)/shard_map/ppermute | solution.py:169
  94.2 3.0 %product.2 = (f32[64,240]{1,0:T(8,128)S(1)}, f32[64,240]{1,0:T(8,128)S(1)}, f32[64,240]{1,0:T(8,128)S(1)}, f32[64,240]{1,0:T(8,128)S(1)}) custom-call(s32[4]{0:T(128)S(1)} %pad_add_fusion.at_ref, f32[64,32768]{1,0:T(8,128)} %amplitudes_ref.3, f32[64,2048]{1,0:T(8,128)S(1)} %collective-permute-done.21.refs_0_, ...), custom_call_target="tpu_custom_call" | custom-call | tf_op jit(solution)/shard_map/product/pallas_call | solution.py:220
  97.8 1.9 %collective-permute-start.39 = (f32[64,240]{1,0:T(8,128)S(1)}, f32[64,240]{1,0:T(8,128)S(1)}, u32[]{:S(2)}, u32[]{:S(2)}) collective-permute-start(f32[64,240]{1,0:T(8,128)S(1)} %get-tuple-element.91), channel_id=1, source_target_pairs={{0,24},{8,0},{16,8},{24,16},{1,25},{9,1},{17,9},{25,17},{2,26},{10... | collective-permute-start | bytes 184328 | tf_op jit(solution)/shard_map/ppermute | solution.py:169
  99.9 1.3 %collective-permute-start.41 = (f32[64,240]{1,0:T(8,128)S(1)}, f32[64,240]{1,0:T(8,128)S(1)}, u32[]{:S(2)}, u32[]{:S(2)}) collective-permute-start(f32[64,240]{1,0:T(8,128)S(1)} %get-tuple-element.93), channel_id=1, source_target_pairs={{0,16},{8,24},{16,0},{24,8},{1,17},{9,25},{17,1},{25,9},{2,18},{10... | collective-permute-start | bytes 184328 | tf_op jit(solution)/shard_map/ppermute | solution.py:169
  101.2 0.9 collective-permute-done.39.b_ref
  102.1 3.8 %collective-permute-done.40.c_ref = f32[64,240]{1,0:T(8,128)S(1)} collective-permute-done((f32[64,240]{1,0:T(8,128)S(1)}, f32[64,240]{1,0:T(8,128)S(1)}, u32[]{:S(2)}, u32[]{:S(2)}) %collective-permute-start.40) | collective-permute-done | bytes 61472 | tf_op jit(solution)/shard_map/ppermute | solution.py:169
  106.6 1.6 %sum.2.a_ref = f32[64,240]{1,0:T(8,128)} custom-call(f32[64,240]{1,0:T(8,128)} %copy-done.3, f32[64,240]{1,0:T(8,128)} %copy-done.10, f32[64,240]{1,0:T(8,128)} %copy-done.11, f32[64,240]{1,0:T(8,128)} %copy-done.12), custom_call_target="tpu_custom_call" | custom-call | tf_op jit(solution)/shard_map/sum/pallas_call | solution.py:237
  108.1 1.5 %collective-permute-start.42 = (f32[64,240]{1,0:T(8,128)}, f32[64,240]{1,0:T(8,128)S(1)}, u32[]{:S(2)}, u32[]{:S(2)}) collective-permute-start(f32[64,240]{1,0:T(8,128)} %sum.2.a_ref), channel_id=1, source_target_pairs={{0,1},{1,2},{2,3},{3,0},{4,5},{5,6},{6,7},{7,4},{8,9},{9,10},{10,1... | collective-permute-start | bytes 184328 | tf_op jit(solution)/shard_map/ppermute | solution.py:169
  110.2 2.1 %collective-permute-start.44 = (f32[64,240]{1,0:T(8,128)}, f32[64,240]{1,0:T(8,128)S(1)}, u32[]{:S(2)}, u32[]{:S(2)}) collective-permute-start(f32[64,240]{1,0:T(8,128)} %sum.2.a_ref), channel_id=1, source_target_pairs={{0,2},{1,3},{2,0},{3,1},{4,6},{5,7},{6,4},{7,5},{8,10},{9,11},{10,... | collective-permute-start | bytes 184328 | tf_op jit(solution)/shard_map/ppermute | solution.py:169
  112.3 0.9 collective-permute-done.42.b_ref
  113.2 0.9 collective-permute-done.43.c_ref
  114.1 2.0 %collective-permute-done.44.d_ref = f32[64,240]{1,0:T(8,128)S(1)} collective-permute-done((f32[64,240]{1,0:T(8,128)}, f32[64,240]{1,0:T(8,128)S(1)}, u32[]{:S(2)}, u32[]{:S(2)}) %collective-permute-start.44) | collective-permute-done | bytes 61472 | tf_op jit(solution)/shard_map/ppermute | solution.py:169
  116.1 0.8 copy-done.2
  117.0 0.8 expand.2
  118.4 0.6 copy-done.5
  (43 shorter events, 3.9 us)
Async XLA Ops:
  0.0 94.2 %copy-start.6 = (s32[4096]{0:T(1024)S(1)}, s32[4096]{0:T(1024)}, u32[]{:S(2)}) copy-start(s32[4096]{0:T(1024)} %param.9) | copy-start | bytes 49156
  3.7 8.5 %collective-permute-start.25 = (f32[240,128]{1,0:T(8,128)S(1)}, f32[240,128]{1,0:T(8,128)S(1)}, u32[]{:S(2)}, u32[]{:S(2)}) collective-permute-start(f32[240,128]{1,0:T(8,128)S(1)} %compact.2.refs_3_), channel_id=1, source_target_pairs={{0,224},{32,0},{64,32},{96,64},{128,96},{160,128},{192,160},{224,1... | collective-permute-start | bytes 368648 | tf_op jit(solution)/shard_map/ppermute | solution.py:169
  9.7 6.3 %collective-permute-start.33 = (f32[240,128]{1,0:T(8,128)S(1)}, f32[240,128]{1,0:T(8,128)S(1)}, u32[]{:S(2)}, u32[]{:S(2)}) collective-permute-start(f32[240,128]{1,0:T(8,128)S(1)} %compact.2.refs_3_), channel_id=1, source_target_pairs={{0,32},{32,64},{64,96},{96,128},{128,160},{160,192},{192,224},{224... | collective-permute-start | bytes 368648 | tf_op jit(solution)/shard_map/ppermute | solution.py:169
  9.7 56.6 %collective-permute-start.24 = (f32[240,128]{1,0:T(8,128)S(1)}, f32[240,128]{1,0:T(8,128)S(1)}, u32[]{:S(2)}, u32[]{:S(2)}) collective-permute-start(f32[240,128]{1,0:T(8,128)S(1)} %compact.2.refs_3_), channel_id=1, source_target_pairs={{0,4},{4,0},{1,5},{5,1},{2,6},{6,2},{3,7},{7,3},{8,12},{12,8},{9,1... | collective-permute-start | bytes 368648 | tf_op jit(solution)/shard_map/ppermute | solution.py:169
  12.3 55.7 %collective-permute-start.27 = (f32[240,128]{1,0:T(8,128)S(1)}, f32[240,128]{1,0:T(8,128)S(1)}, u32[]{:S(2)}, u32[]{:S(2)}) collective-permute-start(f32[240,128]{1,0:T(8,128)S(1)} %collective-permute-done.25.refs_5_), channel_id=1, source_target_pairs={{0,224},{32,0},{64,32},{96,64},{128,96},{160,128},{192,160},{224,1... | collective-permute-start | bytes 368648 | tf_op jit(solution)/shard_map/ppermute | solution.py:169
  15.9 53.7 %collective-permute-start.34 = (f32[240,128]{1,0:T(8,128)S(1)}, f32[240,128]{1,0:T(8,128)S(1)}, u32[]{:S(2)}, u32[]{:S(2)}) collective-permute-start(f32[240,128]{1,0:T(8,128)S(1)} %collective-permute-done.33.refs_17_), channel_id=1, source_target_pairs={{0,32},{32,64},{64,96},{96,128},{128,160},{160,192},{192,224},{224... | collective-permute-start | bytes 368648 | tf_op jit(solution)/shard_map/ppermute | solution.py:169
  16.0 55.7 %collective-permute-start.26 = (f32[240,128]{1,0:T(8,128)S(1)}, f32[240,128]{1,0:T(8,128)S(1)}, u32[]{:S(2)}, u32[]{:S(2)}) collective-permute-start(f32[240,128]{1,0:T(8,128)S(1)} %collective-permute-done.25.refs_5_), channel_id=1, source_target_pairs={{0,4},{4,0},{1,5},{5,1},{2,6},{6,2},{3,7},{7,3},{8,12},{12,8},{9,1... | collective-permute-start | bytes 368648 | tf_op jit(solution)/shard_map/ppermute | solution.py:169
  16.0 58.9 %collective-permute-start.38 = (f32[240,128]{1,0:T(8,128)S(1)}, f32[240,128]{1,0:T(8,128)S(1)}, u32[]{:S(2)}, u32[]{:S(2)}) collective-permute-start(f32[240,128]{1,0:T(8,128)S(1)} %collective-permute-done.33.refs_17_), channel_id=1, source_target_pairs={{0,4},{4,0},{1,5},{5,1},{2,6},{6,2},{3,7},{7,3},{8,12},{12,8},{9,1... | collective-permute-start | bytes 368648 | tf_op jit(solution)/shard_map/ppermute | solution.py:169
  66.3 51.5 %copy-start.4 = (f32[128,1536]{1,0:T(8,128)S(1)}, f32[128,1536]{1,0:T(8,128)}, u32[]{:S(2)}) copy-start(f32[128,1536]{1,0:T(8,128)} %integrals_ref.1) | copy-start | bytes 2359300
  66.3 51.5 %copy-start.13 = (s32[128]{0:T(128)S(1)}, s32[128]{0:T(128)}, u32[]{:S(2)}) copy-start(s32[128]{0:T(128)} %param.10) | copy-start | bytes 1540
  66.3 21.7 %collective-permute-start.21 = (f32[64,2048]{1,0:T(8,128)}, f32[64,2048]{1,0:T(8,128)S(1)}, u32[]{:S(2)}, u32[]{:S(2)}) collective-permute-start(f32[64,2048]{1,0:T(8,128)} %get-tuple-element.86), channel_id=1, source_target_pairs={{0,8},{8,16},{16,24},{24,0},{1,9},{9,17},{17,25},{25,1},{2,10},{10... | collective-permute-start | bytes 1572872 | tf_op jit(solution)/shard_map/ppermute | solution.py:169
  68.0 24.6 %collective-permute-start.22 = (f32[64,2048]{1,0:T(8,128)}, f32[64,2048]{1,0:T(8,128)S(1)}, u32[]{:S(2)}, u32[]{:S(2)}) collective-permute-start(f32[64,2048]{1,0:T(8,128)} %get-tuple-element.87), channel_id=1, source_target_pairs={{0,24},{8,0},{16,8},{24,16},{1,25},{9,1},{17,9},{25,17},{2,26},{10... | collective-permute-start | bytes 1572872 | tf_op jit(solution)/shard_map/ppermute | solution.py:169
  69.6 24.6 %collective-permute-start.23 = (f32[64,2048]{1,0:T(8,128)}, f32[64,2048]{1,0:T(8,128)S(1)}, u32[]{:S(2)}, u32[]{:S(2)}) collective-permute-start(f32[64,2048]{1,0:T(8,128)} %get-tuple-element.88), channel_id=1, source_target_pairs={{0,16},{8,24},{16,0},{24,8},{1,17},{9,25},{17,1},{25,9},{2,18},{10... | collective-permute-start | bytes 1572872 | tf_op jit(solution)/shard_map/ppermute | solution.py:169
  71.6 5.7 %collective-permute-start.29 = (f32[240,128]{1,0:T(8,128)S(1)}, f32[240,128]{1,0:T(8,128)S(1)}, u32[]{:S(2)}, u32[]{:S(2)}) collective-permute-start(f32[240,128]{1,0:T(8,128)S(1)} %collective-permute-done.27.refs_7_), channel_id=1, source_target_pairs={{0,224},{32,0},{64,32},{96,64},{128,96},{160,128},{192,160},{224,1... | collective-permute-start | bytes 368648 | tf_op jit(solution)/shard_map/ppermute | solution.py:169
  74.9 6.1 %collective-permute-start.35 = (f32[240,128]{1,0:T(8,128)S(1)}, f32[240,128]{1,0:T(8,128)S(1)}, u32[]{:S(2)}, u32[]{:S(2)}) collective-permute-start(f32[240,128]{1,0:T(8,128)S(1)} %collective-permute-done.34.refs_15_), channel_id=1, source_target_pairs={{0,32},{32,64},{64,96},{96,128},{128,160},{160,192},{192,224},{224... | collective-permute-start | bytes 368648 | tf_op jit(solution)/shard_map/ppermute | solution.py:169
  77.3 3.7 %collective-permute-start.28 = (f32[240,128]{1,0:T(8,128)S(1)}, f32[240,128]{1,0:T(8,128)S(1)}, u32[]{:S(2)}, u32[]{:S(2)}) collective-permute-start(f32[240,128]{1,0:T(8,128)S(1)} %collective-permute-done.27.refs_7_), channel_id=1, source_target_pairs={{0,4},{4,0},{1,5},{5,1},{2,6},{6,2},{3,7},{7,3},{8,12},{12,8},{9,1... | collective-permute-start | bytes 368648 | tf_op jit(solution)/shard_map/ppermute | solution.py:169
  80.9 1.3 %collective-permute-start.37 = (f32[240,128]{1,0:T(8,128)S(1)}, f32[240,128]{1,0:T(8,128)S(1)}, u32[]{:S(2)}, u32[]{:S(2)}) collective-permute-start(f32[240,128]{1,0:T(8,128)S(1)} %collective-permute-done.34.refs_15_), channel_id=1, source_target_pairs={{0,4},{4,0},{1,5},{5,1},{2,6},{6,2},{3,7},{7,3},{8,12},{12,8},{9,1... | collective-permute-start | bytes 368648 | tf_op jit(solution)/shard_map/ppermute | solution.py:169
  81.0 5.7 %collective-permute-start.31 = (f32[240,128]{1,0:T(8,128)S(1)}, f32[240,128]{1,0:T(8,128)S(1)}, u32[]{:S(2)}, u32[]{:S(2)}) collective-permute-start(f32[240,128]{1,0:T(8,128)S(1)} %collective-permute-done.29.refs_9_), channel_id=1, source_target_pairs={{0,224},{32,0},{64,32},{96,64},{128,96},{160,128},{192,160},{224,1... | collective-permute-start | bytes 368648 | tf_op jit(solution)/shard_map/ppermute | solution.py:169
  82.3 4.4 %collective-permute-start.30 = (f32[240,128]{1,0:T(8,128)S(1)}, f32[240,128]{1,0:T(8,128)S(1)}, u32[]{:S(2)}, u32[]{:S(2)}) collective-permute-start(f32[240,128]{1,0:T(8,128)S(1)} %collective-permute-done.29.refs_9_), channel_id=1, source_target_pairs={{0,4},{4,0},{1,5},{5,1},{2,6},{6,2},{3,7},{7,3},{8,12},{12,8},{9,1... | collective-permute-start | bytes 368648 | tf_op jit(solution)/shard_map/ppermute | solution.py:169
  86.7 1.3 %collective-permute-start.36 = (f32[240,128]{1,0:T(8,128)S(1)}, f32[240,128]{1,0:T(8,128)S(1)}, u32[]{:S(2)}, u32[]{:S(2)}) collective-permute-start(f32[240,128]{1,0:T(8,128)S(1)} %collective-permute-done.35.refs_13_), channel_id=1, source_target_pairs={{0,4},{4,0},{1,5},{5,1},{2,6},{6,2},{3,7},{7,3},{8,12},{12,8},{9,1... | collective-permute-start | bytes 368648 | tf_op jit(solution)/shard_map/ppermute | solution.py:169
  86.7 7.5 %collective-permute-start.32 = (f32[240,128]{1,0:T(8,128)S(1)}, f32[240,128]{1,0:T(8,128)S(1)}, u32[]{:S(2)}, u32[]{:S(2)}) collective-permute-start(f32[240,128]{1,0:T(8,128)S(1)} %collective-permute-done.31.refs_11_), channel_id=1, source_target_pairs={{0,4},{4,0},{1,5},{5,1},{2,6},{6,2},{3,7},{7,3},{8,12},{12,8},{9,1... | collective-permute-start | bytes 368648 | tf_op jit(solution)/shard_map/ppermute | solution.py:169
  97.2 0.6 copy-start.3
  97.8 4.3 %collective-permute-start.39 = (f32[64,240]{1,0:T(8,128)S(1)}, f32[64,240]{1,0:T(8,128)S(1)}, u32[]{:S(2)}, u32[]{:S(2)}) collective-permute-start(f32[64,240]{1,0:T(8,128)S(1)} %get-tuple-element.91), channel_id=1, source_target_pairs={{0,24},{8,0},{16,8},{24,16},{1,25},{9,1},{17,9},{25,17},{2,26},{10... | collective-permute-start | bytes 184328 | tf_op jit(solution)/shard_map/ppermute | solution.py:169
  99.7 6.2 %collective-permute-start.40 = (f32[64,240]{1,0:T(8,128)S(1)}, f32[64,240]{1,0:T(8,128)S(1)}, u32[]{:S(2)}, u32[]{:S(2)}) collective-permute-start(f32[64,240]{1,0:T(8,128)S(1)} %get-tuple-element.92), channel_id=1, source_target_pairs={{0,8},{8,16},{16,24},{24,0},{1,9},{9,17},{17,25},{25,1},{2,10},{10... | collective-permute-start | bytes 184328 | tf_op jit(solution)/shard_map/ppermute | solution.py:169
  99.9 6.1 %collective-permute-start.41 = (f32[64,240]{1,0:T(8,128)S(1)}, f32[64,240]{1,0:T(8,128)S(1)}, u32[]{:S(2)}, u32[]{:S(2)}) collective-permute-start(f32[64,240]{1,0:T(8,128)S(1)} %get-tuple-element.93), channel_id=1, source_target_pairs={{0,16},{8,24},{16,0},{24,8},{1,17},{9,25},{17,1},{25,9},{2,18},{10... | collective-permute-start | bytes 184328 | tf_op jit(solution)/shard_map/ppermute | solution.py:169
  102.1 3.8 %copy-start.10 = (f32[64,240]{1,0:T(8,128)}, f32[64,240]{1,0:T(8,128)S(1)}, u32[]{:S(2)}) copy-start(f32[64,240]{1,0:T(8,128)S(1)} %collective-permute-done.39.b_ref) | copy-start | bytes 184324
  105.9 0.6 copy-start.12
  108.1 5.1 %collective-permute-start.42 = (f32[64,240]{1,0:T(8,128)}, f32[64,240]{1,0:T(8,128)S(1)}, u32[]{:S(2)}, u32[]{:S(2)}) collective-permute-start(f32[64,240]{1,0:T(8,128)} %sum.2.a_ref), channel_id=1, source_target_pairs={{0,1},{1,2},{2,3},{3,0},{4,5},{5,6},{6,7},{7,4},{8,9},{9,10},{10,1... | collective-permute-start | bytes 184328 | tf_op jit(solution)/shard_map/ppermute | solution.py:169
  109.6 4.5 %collective-permute-start.43 = (f32[64,240]{1,0:T(8,128)}, f32[64,240]{1,0:T(8,128)S(1)}, u32[]{:S(2)}, u32[]{:S(2)}) collective-permute-start(f32[64,240]{1,0:T(8,128)} %sum.2.a_ref), channel_id=1, source_target_pairs={{0,3},{1,0},{2,1},{3,2},{4,7},{5,4},{6,5},{7,6},{8,11},{9,8},{10,9... | collective-permute-start | bytes 184328 | tf_op jit(solution)/shard_map/ppermute | solution.py:169
  110.2 6.0 %collective-permute-start.44 = (f32[64,240]{1,0:T(8,128)}, f32[64,240]{1,0:T(8,128)S(1)}, u32[]{:S(2)}, u32[]{:S(2)}) collective-permute-start(f32[64,240]{1,0:T(8,128)} %sum.2.a_ref), channel_id=1, source_target_pairs={{0,2},{1,3},{2,0},{3,1},{4,6},{5,7},{6,4},{7,5},{8,10},{9,11},{10,... | collective-permute-start | bytes 184328 | tf_op jit(solution)/shard_map/ppermute | solution.py:169
  116.1 0.8 copy-start.2
  118.4 0.6 copy-start.5
  (1 other events, 0.6 us)

commit v2 on v0

v2 whole, which is shorter than its diff:
```python
import jax
import jax.numpy as jnp
from jax import lax
from jax.experimental import pallas as pl
from jax.experimental.pallas import tpu as pltpu
from jax.sharding import Mesh
from jax.sharding import PartitionSpec as P

Z, Y, C, X = 8, 4, 2, 4
IRREPS = 8
ROW_DEV = 64
AB_DEV = 128
CD = 1536
CD_DEV = CD // X
LANES = 128
CHUNKS = CD // LANES
CHUNKS_DEV = CD_DEV // LANES
SLOTS = 72
LABEL = X * SLOTS
WIDTH = LABEL + 8
BLOCKS = Z * C
AB_GROUP = BLOCKS * AB_DEV
SHIFTS = (0, 1, Y - 1, 2)
VMEM = pl.BlockSpec(memory_space=pltpu.VMEM)
SMEM = pl.BlockSpec(memory_space=pltpu.SMEM)
ANY = pl.BlockSpec(memory_space=pl.ANY)
PARAMS = pltpu.CompilerParams(vmem_limit_bytes=24 * 2**20)
WHOLE = pltpu.CompilerParams(vmem_limit_bytes=58 * 2**20)
NT = (((1,), (1,)), ((), ()))
NN = (((1,), (0,)), ((), ()))


def split(value):
    high = value.astype(jnp.bfloat16)
    low = (value - high.astype(jnp.float32)).astype(jnp.bfloat16)
    return high, low


def place():
    return [lax.axis_index(axis) for axis in ("z", "y", "c", "x")]


def one_hot(rank, offset):
    slot = lax.broadcasted_iota(jnp.int32, (SLOTS, rank.shape[1]), 0)
    return jnp.where(slot == rank - offset, 1.0, 0.0).astype(jnp.bfloat16)


def label_column(row):
    return jnp.broadcast_to(row.astype(jnp.float32), (LANES, LANES)).T


def find_ranks(slab_ref, rank_ref):
    kinds = lax.broadcasted_iota(jnp.int32, (IRREPS, LANES), 0)
    mine = [slab_ref[k : k + 1, :] == kinds for k in range(CHUNKS)]
    ones = jnp.concatenate([jnp.where(m, 1.0, 0.0) for m in mine], axis=0).astype(jnp.bfloat16)
    row = lax.broadcasted_iota(jnp.int32, (LANES, 2 * LANES), 0)
    column = lax.broadcasted_iota(jnp.int32, (LANES, 2 * LANES), 1)
    upper = jnp.where(row <= column, 1.0, 0.0).astype(jnp.bfloat16)
    counts = lax.dot_general(ones, upper, NN, preferred_element_type=jnp.float32)
    most = jnp.zeros((IRREPS, LANES), jnp.float32)
    for k in range(CHUNKS):
        if k % CHUNKS_DEV == 0:
            before = jnp.zeros((IRREPS, LANES), jnp.float32)
        count = counts[k * IRREPS : (k + 1) * IRREPS]
        place_in = jnp.where(mine[k], before + count[:, :LANES], 0.0)
        rank_ref[k : k + 1, :] = jnp.sum(place_in, axis=0, keepdims=True).astype(jnp.int32) - 1
        before = before + count[:, LANES:]
        most = jnp.maximum(most, before)
    return jnp.max(most).astype(jnp.int32)


def compact(offset, integrals_ref, pair_ref, slab_ref, rank_ref, out_ref):
    labels = label_column(pair_ref[...])
    for q in range(X):
        kept, chosen = [], []
        for k in range(q * CHUNKS_DEV, (q + 1) * CHUNKS_DEV):
            slab = slab_ref[k : k + 1, :].astype(jnp.float32)
            value = integrals_ref[:, k * LANES : (k + 1) * LANES]
            kept.append(jnp.where(labels == slab, value, 0.0))
            chosen.append(one_hot(rank_ref[k : k + 1, :], offset))
        high, low = split(jnp.concatenate(kept, axis=1))
        chosen = jnp.concatenate(chosen, axis=1)
        packed = lax.dot_general(chosen, high, NT, preferred_element_type=jnp.float32)
        packed += lax.dot_general(chosen, low, NT, preferred_element_type=jnp.float32)
        out_ref[q * SLOTS : (q + 1) * SLOTS, :] = packed
    out_ref[LABEL:WIDTH, :] = jnp.broadcast_to(pair_ref[...].astype(jnp.float32), (8, LANES))


def own_columns(amplitudes_ref, out_ref, sems, target, first=0):
    x = lax.axis_index("x")
    copies = []
    for block in range(out_ref.shape[1] // AB_DEV):
        bz, bc = divmod(first + block, C)
        source = pl.multiple_of((((bz * Y + target) * C + bc) * X + x) * AB_DEV, AB_DEV)
        copy = pltpu.make_async_copy(
            amplitudes_ref.at[:, pl.ds(source, AB_DEV)],
            out_ref.at[:, pl.ds(block * AB_DEV, AB_DEV)],
            sems.at[block],
        )
        copy.start()
        copies.append(copy)
    return copies


def select_kernel(amplitudes_ref, up_ref, down_ref, own_ref, sems):
    y = lax.axis_index("y")
    far, near, half = pl.ds(AB_GROUP, AB_GROUP // 2), pl.ds(0, AB_GROUP), BLOCKS // 2
    copies = own_columns(amplitudes_ref, up_ref.at[:, near], sems.at[0], lax.rem(y + 1, Y))
    copies += own_columns(amplitudes_ref, down_ref.at[:, near], sems.at[1], lax.rem(y + Y - 1, Y))
    copies += own_columns(amplitudes_ref, up_ref.at[:, far], sems.at[2], lax.rem(y + 2, Y))
    copies += own_columns(amplitudes_ref, down_ref.at[:, far], sems.at[3], lax.rem(y + 2, Y), half)
    copies += own_columns(amplitudes_ref, own_ref, sems.at[4], y)
    for copy in copies:
        copy.wait()


def compact_kernel(round_ref, integrals_ref, pair_ref, slab_ref, out_ref, rank_ref, rounds_ref):
    most = find_ranks(slab_ref, rank_ref)
    rounds_ref[0] = lax.div(most + (SLOTS - 1), SLOTS)
    compact(round_ref[0] * SLOTS, integrals_ref, pair_ref, slab_ref, rank_ref, out_ref)


def split_kernel(own_ref, up_ref, down_ref, far_up_ref, far_down_ref, high_ref, low_ref):
    half = AB_GROUP // 2
    for d, ref in enumerate((own_ref, up_ref, down_ref)):
        row = pl.ds(d * ROW_DEV, ROW_DEV)
        high_ref[row, :], low_ref[row, :] = split(ref[:, :AB_GROUP])
    row = pl.ds(3 * ROW_DEV, ROW_DEV)
    high_ref[row, :half], low_ref[row, :half] = split(far_up_ref[...])
    high_ref[row, half:], low_ref[row, half:] = split(far_down_ref[...])


def row_labels(rows_ref, z, y, c):
    both = label_column(rows_ref[pl.ds(z * Y + y, 1), :])
    return jnp.where(c == 0, both[:ROW_DEV], both[ROW_DEV:])


def masked_product(high_ref, low_ref, blocks, other, rows_ref, thigh, tlow, vhigh, vlow):
    z, y, c, x = place()
    core = lax.rem(c + other, C)
    columns = []
    for k, block in enumerate(blocks):
        at = pl.ds(k * AB_DEV, AB_DEV)
        for q in range(X):
            high, low = split(block[q * SLOTS : (q + 1) * SLOTS, :])
            vhigh[q * LANES : q * LANES + SLOTS, at] = high
            vlow[q * LANES : q * LANES + SLOTS, at] = low
        columns.append(block[LABEL : LABEL + 1, :])
    for d, shift in enumerate(SHIFTS):
        labels = row_labels(rows_ref, z, lax.rem(y - shift + Y, Y), c)
        rows = pl.ds(d * ROW_DEV, ROW_DEV)
        for k in range(Z):
            at = pl.ds(pl.multiple_of((lax.rem(z + k, Z) * C + core) * AB_DEV, AB_DEV), AB_DEV)
            to = pl.ds(k * AB_DEV, AB_DEV)
            mask = jnp.where(labels == columns[k], 1.0, 0.0).astype(jnp.bfloat16)
            thigh[rows, to] = high_ref[rows, at] * mask
            tlow[rows, to] = low_ref[rows, at] * mask
    total = lax.dot_general(thigh[...], vhigh[...], NT, preferred_element_type=jnp.float32)
    total += lax.dot_general(thigh[...], vlow[...], NT, preferred_element_type=jnp.float32)
    total += lax.dot_general(tlow[...], vhigh[...], NT, preferred_element_type=jnp.float32)
    return total


def own_product_kernel(high_ref, low_ref, *refs):
    blocks = refs[:Z]
    rows_ref, out_ref, *scratch = refs[Z:]
    out_ref[...] = masked_product(high_ref, low_ref, blocks, 0, rows_ref, *scratch)


def product_kernel(high_ref, low_ref, *refs):
    blocks = refs[:Z]
    rows_ref, sum_ref, out_ref, *scratch = refs[Z:]
    z, y, c, x = place()
    total = sum_ref[...] + masked_product(high_ref, low_ref, blocks, 1, rows_ref, *scratch)
    for d, shift in enumerate(SHIFTS):
        target = lax.rem(y - shift + Y, Y)
        for q in range(X):
            out_ref[target * X + q] = total[d * ROW_DEV : (d + 1) * ROW_DEV, q * LANES : q * LANES + SLOTS]


def expand_kernel(round_ref, parts_ref, rows_ref, slab_ref, rank_ref, out_ref):
    z, y, c, x = place()
    total = parts_ref[0]
    for k in range(1, Y * X):
        total += parts_ref[k]
    high = total.astype(jnp.bfloat16)
    middle, low = split(total - high.astype(jnp.float32))
    labels = row_labels(rows_ref, z, y, c)
    for k in range(CHUNKS_DEV):
        at = pl.ds(x * CHUNKS_DEV + k, 1)
        chosen = one_hot(rank_ref[at, :], round_ref[0] * SLOTS)
        wide = lax.dot_general(high, chosen, NN, preferred_element_type=jnp.float32)
        wide += lax.dot_general(middle, chosen, NN, preferred_element_type=jnp.float32)
        wide += lax.dot_general(low, chosen, NN, preferred_element_type=jnp.float32)
        slab = slab_ref[at, :].astype(jnp.float32)
        out_ref[:, k * LANES : (k + 1) * LANES] = jnp.where(labels == slab, wide, 0.0)


def shifted(value, axis, by):
    size = {"z": Z, "y": Y, "c": C, "x": X}[axis]
    return lax.ppermute(value, axis, [(i, (i + by) % size) for i in range(size)])


def f32(*shape):
    return jax.ShapeDtypeStruct(shape, jnp.float32)


def i32(*shape):
    return jax.ShapeDtypeStruct(shape, jnp.int32)


def per_device(amplitudes, integrals, row_irrep, pair_irrep, slab_irrep):
    rows = row_irrep.reshape(-1, LANES)
    pair = pair_irrep.reshape(1, AB_DEV)
    slab = slab_irrep.reshape(CHUNKS, LANES)
    *pieces, own = pl.pallas_call(
        select_kernel,
        out_shape=[f32(ROW_DEV, AB_GROUP * 3 // 2)] * 2 + [f32(ROW_DEV, AB_GROUP)],
        in_specs=[ANY],
        out_specs=[VMEM] * 3,
        scratch_shapes=[pltpu.SemaphoreType.DMA((Y + 1, BLOCKS))],
        compiler_params=WHOLE,
        name="select",
    )(amplitudes)
    near = [shifted(piece, "y", shift) for piece, shift in zip(pieces, (1, -1))]
    far = [shifted(piece[:, AB_GROUP:], "y", shift) for piece, shift in zip(near, (1, -1))]
    halves = pl.pallas_call(
        split_kernel,
        out_shape=[jax.ShapeDtypeStruct((Y * ROW_DEV, AB_GROUP), jnp.bfloat16)] * 2,
        in_specs=[VMEM] * 5,
        out_specs=[VMEM] * 2,
        compiler_params=PARAMS,
        name="split",
    )(own, *near, *far)

    def pack(number):
        return pl.pallas_call(
            compact_kernel,
            out_shape=[f32(WIDTH, AB_DEV), i32(CHUNKS, LANES), i32(1)],
            in_specs=[SMEM] + [VMEM] * 3,
            out_specs=[VMEM, VMEM, SMEM],
            compiler_params=PARAMS,
            name="compact",
        )(number.reshape(1), integrals, pair, slab)

    def ladder_round(number, packed, rank):
        blocks = {0: packed}
        up = down = packed
        for step in range(1, Z // 2 + 1):
            up = shifted(up, "z", -1)
            blocks[step] = up
            if step < Z // 2:
                down = shifted(down, "z", 1)
                blocks[Z - step] = down
        scratch = [
            pltpu.VMEM((Y * ROW_DEV, Z * AB_DEV), jnp.bfloat16),
            pltpu.VMEM((Y * ROW_DEV, Z * AB_DEV), jnp.bfloat16),
            pltpu.VMEM((X * LANES, Z * AB_DEV), jnp.bfloat16),
            pltpu.VMEM((X * LANES, Z * AB_DEV), jnp.bfloat16),
        ]
        blocks = [blocks[step] for step in range(Z)]
        others = [shifted(block, "c", 1) for block in blocks]
        partial = pl.pallas_call(
            own_product_kernel,
            out_shape=f32(Y * ROW_DEV, X * LANES),
            in_specs=[VMEM] * (2 + Z + 1),
            out_specs=VMEM,
            scratch_shapes=scratch,
            compiler_params=PARAMS,
            name="own_product",
        )(*halves, *blocks, rows)
        parts = pl.pallas_call(
            product_kernel,
            out_shape=f32(Y * X, ROW_DEV, SLOTS),
            in_specs=[VMEM] * (4 + Z),
            out_specs=VMEM,
            scratch_shapes=scratch,
            compiler_params=PARAMS,
            name="product",
        )(*halves, *others, rows, partial)
        parts = lax.all_to_all(parts, ("y", "x"), split_axis=0, concat_axis=0, tiled=True)
        return pl.pallas_call(
            expand_kernel,
            out_shape=f32(ROW_DEV, CD_DEV),
            in_specs=[SMEM] + [VMEM] * 4,
            out_specs=VMEM,
            compiler_params=PARAMS,
            name="expand",
        )(number.reshape(1), parts, rows, slab, rank)

    def extra_round(state):
        number, ladder = state
        packed, rank, _ = pack(number)
        return number + 1, ladder + ladder_round(number, packed, rank)

    number = jnp.zeros((), jnp.int32)
    packed, rank, rounds = pack(number)
    first = ladder_round(number, packed, rank)
    _, ladder = lax.while_loop(lambda state: state[0] < rounds[0], extra_round, (number + 1, first))
    return ladder


def solution(mesh):
    grid = Mesh(mesh.devices.reshape(Z, Y, C, X), ("z", "y", "c", "x"))
    placed = (P(("z", "y", "c"), None), P(("z", "y", "c", "x"), None), P(), P(("z", "y", "c", "x")), P())
    return jax.shard_map(
        per_device, mesh=grid, in_specs=placed, out_specs=P(("z", "y", "c"), "x"), check_vma=False
    )
```

time: 487 us -> 65.3 us (0.13)
  waiting for transfers between devices: 367 us -> 21.7 us
  blocking collectives: 63.3 us -> 0 us
  starting transfers between devices: 0.04 us -> 31.4 us
  matrix products: 23.2 us -> 0 us
  local copies, waits for them, and re-layouts: 17.7 us -> 1.73 us
  between operations: 13.5 us -> 0.17 us
  Pallas kernels: 0 us -> 8.77 us
    reduce_scatter x2 -> x0, waiting for transfers between devices: 367 us -> none  [the longest x1 213 us: per_device(): lax.psum_scatter(partial_value, 'rep', scatter_dimension=1, tiled=True)]
    all_to_all x1 -> x0, blocking collectives: 63.3 us -> none  [per_device(): lax.all_to_all(selected, 'pair', split_axis=1, concat_axis=0, tiled=True)]
    ppermute x0 -> x19, starting transfers between devices: none -> 26.4 us  [shifted(): lax.ppermute(value, axis, [(i, (i + by) % size) for i in range(size)])]
    dot_general x1 -> x0, matrix products: 23.2 us -> none  [per_device(): jnp.dot(kept_rows, kept_slab, precision=lax.Precision.HIGHEST, preferred_...]
    ppermute x0 -> x19, waiting for transfers between devices: none -> 11.3 us  [shifted(): lax.ppermute(value, axis, [(i, (i + by) % size) for i in range(size)])]
    reshape x1 -> x0, local copies, waits for them, and re-layouts: 10.8 us -> none  [per_device(): grouped = amplitudes.reshape(row_count, pair_count, rep_count, columns)]
    all_to_all x0 -> x1, waiting for transfers between devices: none -> 10.4 us  [ladder_round(): lax.all_to_all(parts, ('y', 'x'), split_axis=0, concat_axis=0, tiled=True)]
    pallas_call x0 -> x6, Pallas kernels: none -> 8.77 us  [the longest x1 3.66 us: per_device(): pl.pallas_call(select_kernel, out_shape=[f32(ROW_DEV, AB_GROUP * 3 // 2)]...]
  transfers between devices with their start and end apart: 2 -> 20, of which waited for: 2 -> 5; matrix products, arithmetic and copies ran while one was open for 0% -> 0% of each run, Pallas kernels for 0% -> 4%
where the time goes in v2:
time: 65.3 us; the launch traced here: 64.4 us
  starting transfers between devices  31.4 us (48%)
  waiting for transfers between devices  21.7 us (33%)
  Pallas kernels  8.77 us (13%)
  local copies, waits for them, and re-layouts  1.73 us (3%)
    ppermute x19, starting transfers between devices, shifted(): lax.ppermute(value, axis, [(i, (i + by) % size) for i in range(size)])  26.4 us
    ppermute x19, waiting for transfers between devices, shifted(): lax.ppermute(value, axis, [(i, (i + by) % size) for i in range(size)])  11.3 us
    all_to_all x1, waiting for transfers between devices, ladder_round(): lax.all_to_all(parts, ('y', 'x'), split_axis=0, concat_axis=0, tiled=True)  10.4 us
    all_to_all x1, starting transfers between devices, ladder_round(): lax.all_to_all(parts, ('y', 'x'), split_axis=0, concat_axis=0, tiled=True)  4.99 us
    pallas_call x1, Pallas kernels, per_device(): pl.pallas_call(select_kernel, out_shape=[f32(ROW_DEV, AB_GROUP * 3 // 2)]...  3.66 us
    pallas_call x1, Pallas kernels, ladder_round(): pl.pallas_call(product_kernel, out_shape=f32(Y * X, ROW_DEV, SLOTS), in_s...  2.26 us
    unnamed x12, local copies, waits for them, and re-layouts  1.69 us
    pallas_call x1, Pallas kernels, ladder_round(): pl.pallas_call(own_product_kernel, out_shape=f32(Y * ROW_DEV, X * LANES),...  1.45 us
  transfers between devices with their start and end apart: 20, of which 5 were waited for; matrix products, arithmetic and copies ran while one was open for 0% of the time, Pallas kernels for 4%

profile of v2, /device:TPU:2, one launch (start us, length us, event | category | flops | bytes accessed | tf_op | source)
XLA Modules:
  0.0 64.4 jit_solution(3756595450001635684)
XLA Ops:
  0.0 3.7 %select.1 = (f32[64,3072]{1,0:T(8,128)}, f32[64,3072]{1,0:T(8,128)}, f32[64,2048]{1,0:T(8,128)}) custom-call(f32[64,32768]{1,0:T(8,128)} %amplitudes_ref.1), custom_call_target="tpu_custom_call" | custom-call | tf_op jit(solution)/shard_map/select/pallas_call | solution.py:216
  3.7 1.7 %collective-permute-start.15 = (f32[64,3072]{1,0:T(8,128)}, f32[64,3072]{1,0:T(8,128)S(1)}, u32[]{:S(2)}, u32[]{:S(2)}) collective-permute-start(f32[64,3072]{1,0:T(8,128)} %get-tuple-element.64), channel_id=1, source_target_pairs={{0,8},{8,16},{16,24},{24,0},{1,9},{9,17},{17,25},{25,1},{2,10},{10... | collective-permute-start | bytes 2359304 | tf_op jit(solution)/shard_map/ppermute | solution.py:201
  5.3 1.7 %collective-permute-start.16 = (f32[64,3072]{1,0:T(8,128)}, f32[64,3072]{1,0:T(8,128)S(1)}, u32[]{:S(2)}, u32[]{:S(2)}) collective-permute-start(f32[64,3072]{1,0:T(8,128)} %get-tuple-element.65), channel_id=1, source_target_pairs={{0,24},{8,0},{16,8},{24,16},{1,25},{9,1},{17,9},{25,17},{2,26},{10... | collective-permute-start | bytes 2359304 | tf_op jit(solution)/shard_map/ppermute | solution.py:201
  7.0 0.8 %compact.2 = (f32[296,128]{1,0:T(8,128)S(1)}, s32[12,128]{1,0:T(8,128)S(1)}, s32[1]{0:T(128)}) custom-call(s32[1]{0:T(128)} %constant.2.clone.1.round_ref, f32[128,1536]{1,0:T(8,128)S(1)} %copy-done.1, s32[1,128]{1,0:T(1,128)S(1)} %bitcast.15, s32[12,128]{1,0:T(8,128)S(1)} %bitcast.12), custom_call_target="tpu_custom_call" | custom-call | tf_op jit(solution)/shard_map/compact/pallas_call | solution.py:237
  7.9 5.9 %collective-permute-start.20 = (f32[296,128]{1,0:T(8,128)S(1)}, f32[296,128]{1,0:T(8,128)S(1)}, u32[]{:S(2)}, u32[]{:S(2)}) collective-permute-start(f32[296,128]{1,0:T(8,128)S(1)} %get-tuple-element.68.refs_0_), channel_id=1, source_target_pairs={{0,224},{32,0},{64,32},{96,64},{128,96},{160,128},{192,160},{224,1... | collective-permute-start | bytes 454664 | tf_op jit(solution)/shard_map/ppermute | solution.py:201
  13.8 0.0 collective-permute-start.28
  13.8 2.8 %collective-permute-done.20.refs_1_ = f32[296,128]{1,0:T(8,128)S(1)} collective-permute-done((f32[296,128]{1,0:T(8,128)S(1)}, f32[296,128]{1,0:T(8,128)S(1)}, u32[]{:S(2)}, u32[]{:S(2)}) %collective-permute-start.20) | collective-permute-done | bytes 151584 | tf_op jit(solution)/shard_map/ppermute | solution.py:201
  16.6 3.7 %collective-permute-start.22 = (f32[296,128]{1,0:T(8,128)S(1)}, f32[296,128]{1,0:T(8,128)S(1)}, u32[]{:S(2)}, u32[]{:S(2)}) collective-permute-start(f32[296,128]{1,0:T(8,128)S(1)} %collective-permute-done.20.refs_1_), channel_id=1, source_target_pairs={{0,224},{32,0},{64,32},{96,64},{128,96},{160,128},{192,160},{224,1... | collective-permute-start | bytes 454664 | tf_op jit(solution)/shard_map/ppermute | solution.py:201
  20.3 2.7 %collective-permute-done.22.refs_2_ = f32[296,128]{1,0:T(8,128)S(1)} collective-permute-done((f32[296,128]{1,0:T(8,128)S(1)}, f32[296,128]{1,0:T(8,128)S(1)}, u32[]{:S(2)}, u32[]{:S(2)}) %collective-permute-start.22) | collective-permute-done | bytes 151584 | tf_op jit(solution)/shard_map/ppermute | solution.py:201
  23.0 1.5 %collective-permute-done.15.up_ref = f32[64,3072]{1,0:T(8,128)S(1)} collective-permute-done((f32[64,3072]{1,0:T(8,128)}, f32[64,3072]{1,0:T(8,128)S(1)}, u32[]{:S(2)}, u32[]{:S(2)}) %collective-permute-start.15) | collective-permute-done | bytes 786464 | tf_op jit(solution)/shard_map/ppermute | solution.py:201
  24.5 5.9 %collective-permute-start.24 = (f32[296,128]{1,0:T(8,128)S(1)}, f32[296,128]{1,0:T(8,128)S(1)}, u32[]{:S(2)}, u32[]{:S(2)}) collective-permute-start(f32[296,128]{1,0:T(8,128)S(1)} %collective-permute-done.22.refs_2_), channel_id=1, source_target_pairs={{0,224},{32,0},{64,32},{96,64},{128,96},{160,128},{192,160},{224,1... | collective-permute-start | bytes 454664 | tf_op jit(solution)/shard_map/ppermute | solution.py:201
  30.4 0.4 collective-permute-start.17
  30.8 2.9 %collective-permute-start.18 = (f32[64,1024]{1,0:T(8,128)S(1)}, f32[64,1024]{1,0:T(8,128)S(1)}, u32[]{:S(2)}, u32[]{:S(2)}) collective-permute-start(f32[64,1024]{1,0:T(8,128)S(1)} %slice.9), channel_id=1, source_target_pairs={{0,24},{8,0},{16,8},{24,16},{1,25},{9,1},{17,9},{25,17},{2,26},{10... | collective-permute-start | bytes 786440 | tf_op jit(solution)/shard_map/ppermute | solution.py:201
  33.8 0.0 collective-permute-done.29.refs_6_
  33.8 0.1 collective-permute-start.30
  33.9 0.0 collective-permute-done.24.refs_3_
  33.9 3.2 %collective-permute-start.26 = (f32[296,128]{1,0:T(8,128)S(1)}, f32[296,128]{1,0:T(8,128)S(1)}, u32[]{:S(2)}, u32[]{:S(2)}) collective-permute-start(f32[296,128]{1,0:T(8,128)S(1)} %collective-permute-done.24.refs_3_), channel_id=1, source_target_pairs={{0,224},{32,0},{64,32},{96,64},{128,96},{160,128},{192,160},{224,1... | collective-permute-start | bytes 454664 | tf_op jit(solution)/shard_map/ppermute | solution.py:201
  37.1 4.2 %collective-permute-done.30.refs_5_ = f32[296,128]{1,0:T(8,128)S(1)} collective-permute-done((f32[296,128]{1,0:T(8,128)S(1)}, f32[296,128]{1,0:T(8,128)S(1)}, u32[]{:S(2)}, u32[]{:S(2)}) %collective-permute-start.30) | collective-permute-done | bytes 151584 | tf_op jit(solution)/shard_map/ppermute | solution.py:201
  41.4 0.0 collective-permute-done.26.refs_4_
  41.4 0.5 collective-permute-start.25
  41.9 0.1 collective-permute-start.31
  42.0 0.4 collective-permute-start.27
  42.4 1.0 %copy-done = f32[64,2048]{1,0:T(8,128)S(1)} copy-done((f32[64,2048]{1,0:T(8,128)S(1)}, f32[64,2048]{1,0:T(8,128)}, u32[]{:S(2)}) %copy-start) | copy-done | bytes 524312
  43.4 0.4 split.1
  43.8 1.5 %own_product.2.refs_9_ = f32[256,512]{1,0:T(8,128)S(1)} custom-call(bf16[256,2048]{1,0:T(8,128)(2,1)S(1)} %get-tuple-element.156.high_ref, bf16[256,2048]{1,0:T(8,128)(2,1)S(1)} %get-tuple-element.157.low_ref, f32[296,128]{1,0:T(8,128)S(1)} %get-tuple-element.68.refs_0_, f32[296,128]{1,0:T(8,128)S(1)} %collective-permute-done.20.refs_1_, ...), custom_call_target="tpu_custom_call" | custom-call | tf_op jit(solution)/shard_map/own_product/pallas_call | solution.py:263
  45.3 2.3 %product.2 = f32[16,64,72]{2,1,0:T(8,128)} custom-call(bf16[256,2048]{1,0:T(8,128)(2,1)S(1)} %get-tuple-element.156.high_ref, bf16[256,2048]{1,0:T(8,128)(2,1)S(1)} %get-tuple-element.157.low_ref, f32[296,128]{1,0:T(8,128)S(1)} %collective-permute-done.19.refs_0_, f32[296,128]{1,0:T(8,128)S(1)} %collective-permute-done.21.refs_1_, ...), custom_call_target="tpu_custom_call" | custom-call | tf_op jit(solution)/shard_map/product/pallas_call | solution.py:272
  47.6 5.0 %all-to-all-start.1 = ((f32[16,64,72]{2,1,0:T(8,128)}), f32[16,64,72]{2,1,0:T(8,128)S(1)}, u32[]{:S(2)}, u32[]{:S(2)}) async-start(f32[16,64,72]{2,1,0:T(8,128)} %product.2), calls=%async_computation.1 | async-start | bytes 1048576 | tf_op jit(solution)/shard_map/all_to_all | solution.py:281
  52.6 10.4 %all-to-all-done.1.parts_ref = f32[16,64,72]{2,1,0:T(8,128)S(1)} async-done(((f32[16,64,72]{2,1,0:T(8,128)}), f32[16,64,72]{2,1,0:T(8,128)S(1)}, u32[]{:S(2)}, u32[]{:S(2)}) %all-to-all-start.1) | async-done | bytes 294944 | tf_op jit(solution)/shard_map/all_to_all | solution.py:281
  63.0 0.2 expand.2
  63.2 0.6 while.10
  63.8 0.0 copy-start.3
  63.8 0.6 copy-done.3
  (29 shorter events, 0.1 us)
Async XLA Ops:
  0.0 7.0 %copy-start.4 = (s32[1536]{0:T(1024)S(1)}, s32[1536]{0:T(1024)}, u32[]{:S(2)}) copy-start(s32[1536]{0:T(1024)} %param.11) | copy-start | bytes 18436
  0.0 7.0 %copy-start.5 = (s32[128]{0:T(128)S(1)}, s32[128]{0:T(128)}, u32[]{:S(2)}) copy-start(s32[128]{0:T(128)} %param.10) | copy-start | bytes 1540
  0.0 7.0 %copy-start.1 = (f32[128,1536]{1,0:T(8,128)S(1)}, f32[128,1536]{1,0:T(8,128)}, u32[]{:S(2)}) copy-start(f32[128,1536]{1,0:T(8,128)} %integrals_ref.1) | copy-start | bytes 2359300
  0.0 43.8 %copy-start.2 = (s32[4096]{0:T(1024)S(1)}, s32[4096]{0:T(1024)}, u32[]{:S(2)}) copy-start(s32[4096]{0:T(1024)} %param.9) | copy-start | bytes 49156
  3.7 20.8 %collective-permute-start.15 = (f32[64,3072]{1,0:T(8,128)}, f32[64,3072]{1,0:T(8,128)S(1)}, u32[]{:S(2)}, u32[]{:S(2)}) collective-permute-start(f32[64,3072]{1,0:T(8,128)} %get-tuple-element.64), channel_id=1, source_target_pairs={{0,8},{8,16},{16,24},{24,0},{1,9},{9,17},{17,25},{25,1},{2,10},{10... | collective-permute-start | bytes 2359304 | tf_op jit(solution)/shard_map/ppermute | solution.py:201
  5.3 25.1 %collective-permute-start.16 = (f32[64,3072]{1,0:T(8,128)}, f32[64,3072]{1,0:T(8,128)S(1)}, u32[]{:S(2)}, u32[]{:S(2)}) collective-permute-start(f32[64,3072]{1,0:T(8,128)} %get-tuple-element.65), channel_id=1, source_target_pairs={{0,24},{8,0},{16,8},{24,16},{1,25},{9,1},{17,9},{25,17},{2,26},{10... | collective-permute-start | bytes 2359304 | tf_op jit(solution)/shard_map/ppermute | solution.py:201
  7.9 8.7 %collective-permute-start.20 = (f32[296,128]{1,0:T(8,128)S(1)}, f32[296,128]{1,0:T(8,128)S(1)}, u32[]{:S(2)}, u32[]{:S(2)}) collective-permute-start(f32[296,128]{1,0:T(8,128)S(1)} %get-tuple-element.68.refs_0_), channel_id=1, source_target_pairs={{0,224},{32,0},{64,32},{96,64},{128,96},{160,128},{192,160},{224,1... | collective-permute-start | bytes 454664 | tf_op jit(solution)/shard_map/ppermute | solution.py:201
  13.8 6.5 %collective-permute-start.28 = (f32[296,128]{1,0:T(8,128)S(1)}, f32[296,128]{1,0:T(8,128)S(1)}, u32[]{:S(2)}, u32[]{:S(2)}) collective-permute-start(f32[296,128]{1,0:T(8,128)S(1)} %get-tuple-element.68.refs_0_), channel_id=1, source_target_pairs={{0,32},{32,64},{64,96},{96,128},{128,160},{160,192},{192,224},{224... | collective-permute-start | bytes 454664 | tf_op jit(solution)/shard_map/ppermute | solution.py:201
  16.6 6.4 %collective-permute-start.22 = (f32[296,128]{1,0:T(8,128)S(1)}, f32[296,128]{1,0:T(8,128)S(1)}, u32[]{:S(2)}, u32[]{:S(2)}) collective-permute-start(f32[296,128]{1,0:T(8,128)S(1)} %collective-permute-done.20.refs_1_), channel_id=1, source_target_pairs={{0,224},{32,0},{64,32},{96,64},{128,96},{160,128},{192,160},{224,1... | collective-permute-start | bytes 454664 | tf_op jit(solution)/shard_map/ppermute | solution.py:201
  20.3 10.6 %collective-permute-start.19 = (f32[296,128]{1,0:T(8,128)S(1)}, f32[296,128]{1,0:T(8,128)S(1)}, u32[]{:S(2)}, u32[]{:S(2)}) collective-permute-start(f32[296,128]{1,0:T(8,128)S(1)} %get-tuple-element.68.refs_0_), channel_id=1, source_target_pairs={{0,4},{4,0},{1,5},{5,1},{2,6},{6,2},{3,7},{7,3},{8,12},{12,8},{9,1... | collective-permute-start | bytes 454664 | tf_op jit(solution)/shard_map/ppermute | solution.py:201
  20.3 13.5 %collective-permute-start.29 = (f32[296,128]{1,0:T(8,128)S(1)}, f32[296,128]{1,0:T(8,128)S(1)}, u32[]{:S(2)}, u32[]{:S(2)}) collective-permute-start(f32[296,128]{1,0:T(8,128)S(1)} %collective-permute-done.28.refs_7_), channel_id=1, source_target_pairs={{0,32},{32,64},{64,96},{96,128},{128,160},{160,192},{192,224},{224... | collective-permute-start | bytes 454664 | tf_op jit(solution)/shard_map/ppermute | solution.py:201
  23.0 10.8 %collective-permute-start.21 = (f32[296,128]{1,0:T(8,128)S(1)}, f32[296,128]{1,0:T(8,128)S(1)}, u32[]{:S(2)}, u32[]{:S(2)}) collective-permute-start(f32[296,128]{1,0:T(8,128)S(1)} %collective-permute-done.20.refs_1_), channel_id=1, source_target_pairs={{0,4},{4,0},{1,5},{5,1},{2,6},{6,2},{3,7},{7,3},{8,12},{12,8},{9,1... | collective-permute-start | bytes 454664 | tf_op jit(solution)/shard_map/ppermute | solution.py:201
  24.5 9.3 %collective-permute-start.24 = (f32[296,128]{1,0:T(8,128)S(1)}, f32[296,128]{1,0:T(8,128)S(1)}, u32[]{:S(2)}, u32[]{:S(2)}) collective-permute-start(f32[296,128]{1,0:T(8,128)S(1)} %collective-permute-done.22.refs_2_), channel_id=1, source_target_pairs={{0,224},{32,0},{64,32},{96,64},{128,96},{160,128},{192,160},{224,1... | collective-permute-start | bytes 454664 | tf_op jit(solution)/shard_map/ppermute | solution.py:201
  30.4 11.4 %collective-permute-start.17 = (f32[64,1024]{1,0:T(8,128)S(1)}, f32[64,1024]{1,0:T(8,128)S(1)}, u32[]{:S(2)}, u32[]{:S(2)}) collective-permute-start(f32[64,1024]{1,0:T(8,128)S(1)} %slice.8), channel_id=1, source_target_pairs={{0,8},{8,16},{16,24},{24,0},{1,9},{9,17},{17,25},{25,1},{2,10},{10... | collective-permute-start | bytes 786440 | tf_op jit(solution)/shard_map/ppermute | solution.py:201
  30.8 11.1 %collective-permute-start.18 = (f32[64,1024]{1,0:T(8,128)S(1)}, f32[64,1024]{1,0:T(8,128)S(1)}, u32[]{:S(2)}, u32[]{:S(2)}) collective-permute-start(f32[64,1024]{1,0:T(8,128)S(1)} %slice.9), channel_id=1, source_target_pairs={{0,24},{8,0},{16,8},{24,16},{1,25},{9,1},{17,9},{25,17},{2,26},{10... | collective-permute-start | bytes 786440 | tf_op jit(solution)/shard_map/ppermute | solution.py:201
  33.8 3.3 %collective-permute-start.33 = (f32[296,128]{1,0:T(8,128)S(1)}, f32[296,128]{1,0:T(8,128)S(1)}, u32[]{:S(2)}, u32[]{:S(2)}) collective-permute-start(f32[296,128]{1,0:T(8,128)S(1)} %collective-permute-done.28.refs_7_), channel_id=1, source_target_pairs={{0,4},{4,0},{1,5},{5,1},{2,6},{6,2},{3,7},{7,3},{8,12},{12,8},{9,1... | collective-permute-start | bytes 454664 | tf_op jit(solution)/shard_map/ppermute | solution.py:201
  33.8 7.6 %collective-permute-start.30 = (f32[296,128]{1,0:T(8,128)S(1)}, f32[296,128]{1,0:T(8,128)S(1)}, u32[]{:S(2)}, u32[]{:S(2)}) collective-permute-start(f32[296,128]{1,0:T(8,128)S(1)} %collective-permute-done.29.refs_6_), channel_id=1, source_target_pairs={{0,32},{32,64},{64,96},{96,128},{128,160},{160,192},{192,224},{224... | collective-permute-start | bytes 454664 | tf_op jit(solution)/shard_map/ppermute | solution.py:201
  33.9 7.5 %collective-permute-start.26 = (f32[296,128]{1,0:T(8,128)S(1)}, f32[296,128]{1,0:T(8,128)S(1)}, u32[]{:S(2)}, u32[]{:S(2)}) collective-permute-start(f32[296,128]{1,0:T(8,128)S(1)} %collective-permute-done.24.refs_3_), channel_id=1, source_target_pairs={{0,224},{32,0},{64,32},{96,64},{128,96},{160,128},{192,160},{224,1... | collective-permute-start | bytes 454664 | tf_op jit(solution)/shard_map/ppermute | solution.py:201
  37.1 8.2 %collective-permute-start.23 = (f32[296,128]{1,0:T(8,128)S(1)}, f32[296,128]{1,0:T(8,128)S(1)}, u32[]{:S(2)}, u32[]{:S(2)}) collective-permute-start(f32[296,128]{1,0:T(8,128)S(1)} %collective-permute-done.22.refs_2_), channel_id=1, source_target_pairs={{0,4},{4,0},{1,5},{5,1},{2,6},{6,2},{3,7},{7,3},{8,12},{12,8},{9,1... | collective-permute-start | bytes 454664 | tf_op jit(solution)/shard_map/ppermute | solution.py:201
  41.4 3.9 %collective-permute-start.32 = (f32[296,128]{1,0:T(8,128)S(1)}, f32[296,128]{1,0:T(8,128)S(1)}, u32[]{:S(2)}, u32[]{:S(2)}) collective-permute-start(f32[296,128]{1,0:T(8,128)S(1)} %collective-permute-done.29.refs_6_), channel_id=1, source_target_pairs={{0,4},{4,0},{1,5},{5,1},{2,6},{6,2},{3,7},{7,3},{8,12},{12,8},{9,1... | collective-permute-start | bytes 454664 | tf_op jit(solution)/shard_map/ppermute | solution.py:201
  41.4 3.9 %collective-permute-start.25 = (f32[296,128]{1,0:T(8,128)S(1)}, f32[296,128]{1,0:T(8,128)S(1)}, u32[]{:S(2)}, u32[]{:S(2)}) collective-permute-start(f32[296,128]{1,0:T(8,128)S(1)} %collective-permute-done.24.refs_3_), channel_id=1, source_target_pairs={{0,4},{4,0},{1,5},{5,1},{2,6},{6,2},{3,7},{7,3},{8,12},{12,8},{9,1... | collective-permute-start | bytes 454664 | tf_op jit(solution)/shard_map/ppermute | solution.py:201
  41.9 3.4 %collective-permute-start.31 = (f32[296,128]{1,0:T(8,128)S(1)}, f32[296,128]{1,0:T(8,128)S(1)}, u32[]{:S(2)}, u32[]{:S(2)}) collective-permute-start(f32[296,128]{1,0:T(8,128)S(1)} %collective-permute-done.30.refs_5_), channel_id=1, source_target_pairs={{0,4},{4,0},{1,5},{5,1},{2,6},{6,2},{3,7},{7,3},{8,12},{12,8},{9,1... | collective-permute-start | bytes 454664 | tf_op jit(solution)/shard_map/ppermute | solution.py:201
  42.0 3.3 %collective-permute-start.27 = (f32[296,128]{1,0:T(8,128)S(1)}, f32[296,128]{1,0:T(8,128)S(1)}, u32[]{:S(2)}, u32[]{:S(2)}) collective-permute-start(f32[296,128]{1,0:T(8,128)S(1)} %collective-permute-done.26.refs_4_), channel_id=1, source_target_pairs={{0,4},{4,0},{1,5},{5,1},{2,6},{6,2},{3,7},{7,3},{8,12},{12,8},{9,1... | collective-permute-start | bytes 454664 | tf_op jit(solution)/shard_map/ppermute | solution.py:201
  42.4 1.0 %copy-start = (f32[64,2048]{1,0:T(8,128)S(1)}, f32[64,2048]{1,0:T(8,128)}, u32[]{:S(2)}) copy-start(f32[64,2048]{1,0:T(8,128)} %get-tuple-element.63.own_ref) | copy-start | bytes 1572868
  47.6 15.4 %all-to-all-start.1 = ((f32[16,64,72]{2,1,0:T(8,128)}), f32[16,64,72]{2,1,0:T(8,128)S(1)}, u32[]{:S(2)}, u32[]{:S(2)}) async-start(f32[16,64,72]{2,1,0:T(8,128)} %product.2), calls=%async_computation.1 | async-start | bytes 1048576 | tf_op jit(solution)/shard_map/all_to_all | solution.py:281
  63.8 0.6 copy-start.3

commit v3 on v2

--- a/solution.py
+++ b/solution.py
@@ -16,6 +16,7 @@
 CHUNKS = CD // LANES
 CHUNKS_DEV = CD_DEV // LANES
 SLOTS = 72
+FOLD = 40
 LABEL = X * SLOTS
 WIDTH = LABEL + 8
 BLOCKS = Z * C
@@ -28,6 +29,7 @@
 WHOLE = pltpu.CompilerParams(vmem_limit_bytes=58 * 2**20)
 NT = (((1,), (1,)), ((), ()))
 NN = (((1,), (0,)), ((), ()))
+TN = (((0,), (0,)), ((), ()))
 
 
 def split(value):
@@ -120,14 +122,19 @@
     compact(round_ref[0] * SLOTS, integrals_ref, pair_ref, slab_ref, rank_ref, out_ref)
 
 
-def split_kernel(own_ref, up_ref, down_ref, far_up_ref, far_down_ref, high_ref, low_ref):
+def split_kernel(own_ref, up_ref, down_ref, far_up_ref, far_down_ref, high_ref, low_ref, own, sem):
+    copy = pltpu.make_async_copy(own_ref, own, sem)
+    copy.start()
     half = AB_GROUP // 2
-    for d, ref in enumerate((own_ref, up_ref, down_ref)):
+    for d, ref in ((1, up_ref), (2, down_ref)):
         row = pl.ds(d * ROW_DEV, ROW_DEV)
         high_ref[row, :], low_ref[row, :] = split(ref[:, :AB_GROUP])
     row = pl.ds(3 * ROW_DEV, ROW_DEV)
     high_ref[row, :half], low_ref[row, :half] = split(far_up_ref[...])
     high_ref[row, half:], low_ref[row, half:] = split(far_down_ref[...])
+    copy.wait()
+    row = pl.ds(0, ROW_DEV)
+    high_ref[row, :], low_ref[row, :] = split(own[...])
 
 
 def row_labels(rows_ref, z, y, c):
@@ -141,10 +148,7 @@
     columns = []
     for k, block in enumerate(blocks):
         at = pl.ds(k * AB_DEV, AB_DEV)
-        for q in range(X):
-            high, low = split(block[q * SLOTS : (q + 1) * SLOTS, :])
-            vhigh[q * LANES : q * LANES + SLOTS, at] = high
-            vlow[q * LANES : q * LANES + SLOTS, at] = low
+        vhigh[:, at], vlow[:, at] = split(block[:LABEL, :])
         columns.append(block[LABEL : LABEL + 1, :])
     for d, shift in enumerate(SHIFTS):
         labels = row_labels(rows_ref, z, lax.rem(y - shift + Y, Y), c)
@@ -155,9 +159,9 @@
             mask = jnp.where(labels == columns[k], 1.0, 0.0).astype(jnp.bfloat16)
             thigh[rows, to] = high_ref[rows, at] * mask
             tlow[rows, to] = low_ref[rows, at] * mask
-    total = lax.dot_general(thigh[...], vhigh[...], NT, preferred_element_type=jnp.float32)
-    total += lax.dot_general(thigh[...], vlow[...], NT, preferred_element_type=jnp.float32)
-    total += lax.dot_general(tlow[...], vhigh[...], NT, preferred_element_type=jnp.float32)
+    total = lax.dot_general(vhigh[...], thigh[...], NT, preferred_element_type=jnp.float32)
+    total += lax.dot_general(vlow[...], thigh[...], NT, preferred_element_type=jnp.float32)
+    total += lax.dot_general(vhigh[...], tlow[...], NT, preferred_element_type=jnp.float32)
     return total
 
 
@@ -175,7 +179,9 @@
     for d, shift in enumerate(SHIFTS):
         target = lax.rem(y - shift + Y, Y)
         for q in range(X):
-            out_ref[target * X + q] = total[d * ROW_DEV : (d + 1) * ROW_DEV, q * LANES : q * LANES + SLOTS]
+            piece = total[q * SLOTS : (q + 1) * SLOTS, d * ROW_DEV : (d + 1) * ROW_DEV]
+            rest = jnp.concatenate([piece[FOLD:], jnp.zeros((2 * FOLD - SLOTS, ROW_DEV), jnp.float32)], axis=0)
+            out_ref[target * X + q] = jnp.concatenate([piece[:FOLD], rest], axis=1)
 
 
 def expand_kernel(round_ref, parts_ref, rows_ref, slab_ref, rank_ref, out_ref):
@@ -183,17 +189,19 @@
     total = parts_ref[0]
     for k in range(1, Y * X):
         total += parts_ref[k]
+    total = jnp.concatenate([total[:, :ROW_DEV], total[: SLOTS - FOLD, ROW_DEV:]], axis=0)
     high = total.astype(jnp.bfloat16)
     middle, low = split(total - high.astype(jnp.float32))
     labels = row_labels(rows_ref, z, y, c)
     for k in range(CHUNKS_DEV):
         at = pl.ds(x * CHUNKS_DEV + k, 1)
+        to = pl.ds(k * LANES, LANES)
         chosen = one_hot(rank_ref[at, :], round_ref[0] * SLOTS)
-        wide = lax.dot_general(high, chosen, NN, preferred_element_type=jnp.float32)
-        wide += lax.dot_general(middle, chosen, NN, preferred_element_type=jnp.float32)
-        wide += lax.dot_general(low, chosen, NN, preferred_element_type=jnp.float32)
+        wide = lax.dot_general(high, chosen, TN, preferred_element_type=jnp.float32)
+        wide += lax.dot_general(middle, chosen, TN, preferred_element_type=jnp.float32)
+        wide += lax.dot_general(low, chosen, TN, preferred_element_type=jnp.float32)
         slab = slab_ref[at, :].astype(jnp.float32)
-        out_ref[:, k * LANES : (k + 1) * LANES] = jnp.where(labels == slab, wide, 0.0)
+        out_ref[:, to] = jnp.where(labels == slab, wide, 0.0)
 
 
 def shifted(value, axis, by):
@@ -222,17 +230,6 @@
         compiler_params=WHOLE,
         name="select",
     )(amplitudes)
-    near = [shifted(piece, "y", shift) for piece, shift in zip(pieces, (1, -1))]
-    far = [shifted(piece[:, AB_GROUP:], "y", shift) for piece, shift in zip(near, (1, -1))]
-    halves = pl.pallas_call(
-        split_kernel,
-        out_shape=[jax.ShapeDtypeStruct((Y * ROW_DEV, AB_GROUP), jnp.bfloat16)] * 2,
-        in_specs=[VMEM] * 5,
-        out_specs=[VMEM] * 2,
-        compiler_params=PARAMS,
-        name="split",
-    )(own, *near, *far)
-
     def pack(number):
         return pl.pallas_call(
             compact_kernel,
@@ -243,7 +240,7 @@
             name="compact",
         )(number.reshape(1), integrals, pair, slab)
 
-    def ladder_round(number, packed, rank):
+    def gather(packed):
         blocks = {0: packed}
         up = down = packed
         for step in range(1, Z // 2 + 1):
@@ -252,17 +249,19 @@
             if step < Z // 2:
                 down = shifted(down, "z", 1)
                 blocks[Z - step] = down
+        return [blocks[step] for step in range(Z)]
+
+    def ladder_round(number, blocks, rank):
+        others = [shifted(block, "c", 1) for block in blocks]
         scratch = [
             pltpu.VMEM((Y * ROW_DEV, Z * AB_DEV), jnp.bfloat16),
             pltpu.VMEM((Y * ROW_DEV, Z * AB_DEV), jnp.bfloat16),
-            pltpu.VMEM((X * LANES, Z * AB_DEV), jnp.bfloat16),
-            pltpu.VMEM((X * LANES, Z * AB_DEV), jnp.bfloat16),
+            pltpu.VMEM((LABEL, Z * AB_DEV), jnp.bfloat16),
+            pltpu.VMEM((LABEL, Z * AB_DEV), jnp.bfloat16),
         ]
-        blocks = [blocks[step] for step in range(Z)]
-        others = [shifted(block, "c", 1) for block in blocks]
         partial = pl.pallas_call(
             own_product_kernel,
-            out_shape=f32(Y * ROW_DEV, X * LANES),
+            out_shape=f32(LABEL, Y * ROW_DEV),
             in_specs=[VMEM] * (2 + Z + 1),
             out_specs=VMEM,
             scratch_shapes=scratch,
@@ -271,7 +270,7 @@
         )(*halves, *blocks, rows)
         parts = pl.pallas_call(
             product_kernel,
-            out_shape=f32(Y * X, ROW_DEV, SLOTS),
+            out_shape=f32(Y * X, FOLD, 2 * ROW_DEV),
             in_specs=[VMEM] * (4 + Z),
             out_specs=VMEM,
             scratch_shapes=scratch,
@@ -289,13 +288,28 @@
         )(number.reshape(1), parts, rows, slab, rank)
 
     def extra_round(state):
-        number, ladder = state
+        number, base = state
         packed, rank, _ = pack(number)
-        return number + 1, ladder + ladder_round(number, packed, rank)
+        return number + 1, base + ladder_round(number, gather(packed), rank)
 
     number = jnp.zeros((), jnp.int32)
     packed, rank, rounds = pack(number)
-    first = ladder_round(number, packed, rank)
+    blocks = gather(packed)
+    near = [shifted(piece, "y", shift) for piece, shift in zip(pieces, (1, -1))]
+    forward = near
+    far = [shifted(piece[:, AB_GROUP:], "y", shift) for piece, shift in zip(forward, (1, -1))]
+    halves = pl.pallas_call(
+        split_kernel,
+        out_shape=[jax.ShapeDtypeStruct((Y * ROW_DEV, AB_GROUP), jnp.bfloat16)] * 2,
+        in_specs=[ANY] + [VMEM] * 4,
+        out_specs=[VMEM] * 2,
+        scratch_shapes=[pltpu.VMEM((ROW_DEV, AB_GROUP), jnp.float32), pltpu.SemaphoreType.DMA],
+        compiler_params=PARAMS,
+        name="split",
+    )(own, *near, *far)
+
+
+    first = ladder_round(number, blocks, rank)
     _, ladder = lax.while_loop(lambda state: state[0] < rounds[0], extra_round, (number + 1, first))
     return ladder
 

time: 65.3 us -> 62.8 us (0.962)
  waiting for transfers between devices: 21.7 us -> 19.6 us
    all_to_all x1, waiting for transfers between devices: 10.4 us -> 8.28 us  [ladder_round(): lax.all_to_all(parts, ('y', 'x'), split_axis=0, concat_axis=0, tiled=True)]
    pallas_call x2, Pallas kernels: 3.71 us -> 3.01 us  [the longest x1 1.92 us: ladder_round(): pl.pallas_call(product_kernel, out_shape=f32(Y * X, FOLD, 2 * ROW_DEV), i...]
where the time goes in v3:
time: 62.8 us; the launch traced here: 61.7 us
  starting transfers between devices  31.4 us (50%)
  waiting for transfers between devices  19.6 us (31%)
  Pallas kernels  8.23 us (13%)
  local copies, waits for them, and re-layouts  1.73 us (3%)
    ppermute x19, starting transfers between devices, shifted(): lax.ppermute(value, axis, [(i, (i + by) % size) for i in range(size)])  26.4 us
    ppermute x19, waiting for transfers between devices, shifted(): lax.ppermute(value, axis, [(i, (i + by) % size) for i in range(size)])  11.3 us
    all_to_all x1, waiting for transfers between devices, ladder_round(): lax.all_to_all(parts, ('y', 'x'), split_axis=0, concat_axis=0, tiled=True)  8.28 us
    all_to_all x1, starting transfers between devices, ladder_round(): lax.all_to_all(parts, ('y', 'x'), split_axis=0, concat_axis=0, tiled=True)  4.99 us
    pallas_call x1, Pallas kernels, per_device(): pl.pallas_call(select_kernel, out_shape=[f32(ROW_DEV, AB_GROUP * 3 // 2)]...  3.66 us
    pallas_call x1, Pallas kernels, ladder_round(): pl.pallas_call(product_kernel, out_shape=f32(Y * X, FOLD, 2 * ROW_DEV), i...  1.92 us
    unnamed x12, local copies, waits for them, and re-layouts  1.69 us
  transfers between devices with their start and end apart: 20, of which 5 were waited for; matrix products, arithmetic and copies ran while one was open for 0% of the time, Pallas kernels for 4%

profile of v3, /device:TPU:2, one launch (start us, length us, event | category | flops | bytes accessed | tf_op | source)
XLA Modules:
  0.0 61.7 jit_solution(1399782248220065337)
XLA Ops:
  0.0 3.7 %select.1 = (f32[64,3072]{1,0:T(8,128)}, f32[64,3072]{1,0:T(8,128)}, f32[64,2048]{1,0:T(8,128)}) custom-call(f32[64,32768]{1,0:T(8,128)} %amplitudes_ref.1), custom_call_target="tpu_custom_call" | custom-call | tf_op jit(solution)/shard_map/select/pallas_call | solution.py:224
  3.7 1.7 %collective-permute-start.15 = (f32[64,3072]{1,0:T(8,128)}, f32[64,3072]{1,0:T(8,128)S(1)}, u32[]{:S(2)}, u32[]{:S(2)}) collective-permute-start(f32[64,3072]{1,0:T(8,128)} %get-tuple-element.64), channel_id=1, source_target_pairs={{0,8},{8,16},{16,24},{24,0},{1,9},{9,17},{17,25},{25,1},{2,10},{10... | collective-permute-start | bytes 2359304 | tf_op jit(solution)/shard_map/ppermute | solution.py:209
  5.3 1.7 %collective-permute-start.16 = (f32[64,3072]{1,0:T(8,128)}, f32[64,3072]{1,0:T(8,128)S(1)}, u32[]{:S(2)}, u32[]{:S(2)}) collective-permute-start(f32[64,3072]{1,0:T(8,128)} %get-tuple-element.65), channel_id=1, source_target_pairs={{0,24},{8,0},{16,8},{24,16},{1,25},{9,1},{17,9},{25,17},{2,26},{10... | collective-permute-start | bytes 2359304 | tf_op jit(solution)/shard_map/ppermute | solution.py:209
  7.0 0.8 %compact.2 = (f32[296,128]{1,0:T(8,128)S(1)}, s32[12,128]{1,0:T(8,128)S(1)}, s32[1]{0:T(128)}) custom-call(s32[1]{0:T(128)} %constant.2.clone.1.round_ref, f32[128,1536]{1,0:T(8,128)S(1)} %copy-done.1, s32[1,128]{1,0:T(1,128)S(1)} %bitcast.15, s32[12,128]{1,0:T(8,128)S(1)} %bitcast.12), custom_call_target="tpu_custom_call" | custom-call | tf_op jit(solution)/shard_map/compact/pallas_call | solution.py:234
  7.9 5.9 %collective-permute-start.20 = (f32[296,128]{1,0:T(8,128)S(1)}, f32[296,128]{1,0:T(8,128)S(1)}, u32[]{:S(2)}, u32[]{:S(2)}) collective-permute-start(f32[296,128]{1,0:T(8,128)S(1)} %get-tuple-element.68.refs_0_), channel_id=1, source_target_pairs={{0,224},{32,0},{64,32},{96,64},{128,96},{160,128},{192,160},{224,1... | collective-permute-start | bytes 454664 | tf_op jit(solution)/shard_map/ppermute | solution.py:209
  13.8 0.0 collective-permute-start.28
  13.8 2.8 %collective-permute-done.20.refs_1_ = f32[296,128]{1,0:T(8,128)S(1)} collective-permute-done((f32[296,128]{1,0:T(8,128)S(1)}, f32[296,128]{1,0:T(8,128)S(1)}, u32[]{:S(2)}, u32[]{:S(2)}) %collective-permute-start.20) | collective-permute-done | bytes 151584 | tf_op jit(solution)/shard_map/ppermute | solution.py:209
  16.6 3.7 %collective-permute-start.22 = (f32[296,128]{1,0:T(8,128)S(1)}, f32[296,128]{1,0:T(8,128)S(1)}, u32[]{:S(2)}, u32[]{:S(2)}) collective-permute-start(f32[296,128]{1,0:T(8,128)S(1)} %collective-permute-done.20.refs_1_), channel_id=1, source_target_pairs={{0,224},{32,0},{64,32},{96,64},{128,96},{160,128},{192,160},{224,1... | collective-permute-start | bytes 454664 | tf_op jit(solution)/shard_map/ppermute | solution.py:209
  20.3 0.0 collective-permute-done.28.refs_7_
  20.3 0.0 collective-permute-start.29
  20.3 2.7 %collective-permute-done.22.refs_2_ = f32[296,128]{1,0:T(8,128)S(1)} collective-permute-done((f32[296,128]{1,0:T(8,128)S(1)}, f32[296,128]{1,0:T(8,128)S(1)}, u32[]{:S(2)}, u32[]{:S(2)}) %collective-permute-start.22) | collective-permute-done | bytes 151584 | tf_op jit(solution)/shard_map/ppermute | solution.py:209
  23.0 0.0 collective-permute-start.21
  23.0 1.5 %collective-permute-done.15.up_ref = f32[64,3072]{1,0:T(8,128)S(1)} collective-permute-done((f32[64,3072]{1,0:T(8,128)}, f32[64,3072]{1,0:T(8,128)S(1)}, u32[]{:S(2)}, u32[]{:S(2)}) %collective-permute-start.15) | collective-permute-done | bytes 786464 | tf_op jit(solution)/shard_map/ppermute | solution.py:209
  24.5 5.9 %collective-permute-start.24 = (f32[296,128]{1,0:T(8,128)S(1)}, f32[296,128]{1,0:T(8,128)S(1)}, u32[]{:S(2)}, u32[]{:S(2)}) collective-permute-start(f32[296,128]{1,0:T(8,128)S(1)} %collective-permute-done.22.refs_2_), channel_id=1, source_target_pairs={{0,224},{32,0},{64,32},{96,64},{128,96},{160,128},{192,160},{224,1... | collective-permute-start | bytes 454664 | tf_op jit(solution)/shard_map/ppermute | solution.py:209
  30.4 0.4 collective-permute-start.17
  30.8 2.9 %collective-permute-start.18 = (f32[64,1024]{1,0:T(8,128)S(1)}, f32[64,1024]{1,0:T(8,128)S(1)}, u32[]{:S(2)}, u32[]{:S(2)}) collective-permute-start(f32[64,1024]{1,0:T(8,128)S(1)} %slice.9), channel_id=1, source_target_pairs={{0,24},{8,0},{16,8},{24,16},{1,25},{9,1},{17,9},{25,17},{2,26},{10... | collective-permute-start | bytes 786440 | tf_op jit(solution)/shard_map/ppermute | solution.py:209
  33.8 0.1 collective-permute-start.30
  33.9 3.2 %collective-permute-start.26 = (f32[296,128]{1,0:T(8,128)S(1)}, f32[296,128]{1,0:T(8,128)S(1)}, u32[]{:S(2)}, u32[]{:S(2)}) collective-permute-start(f32[296,128]{1,0:T(8,128)S(1)} %collective-permute-done.24.refs_3_), channel_id=1, source_target_pairs={{0,224},{32,0},{64,32},{96,64},{128,96},{160,128},{192,160},{224,1... | collective-permute-start | bytes 454664 | tf_op jit(solution)/shard_map/ppermute | solution.py:209
  37.1 4.2 %collective-permute-done.30.refs_5_ = f32[296,128]{1,0:T(8,128)S(1)} collective-permute-done((f32[296,128]{1,0:T(8,128)S(1)}, f32[296,128]{1,0:T(8,128)S(1)}, u32[]{:S(2)}, u32[]{:S(2)}) %collective-permute-start.30) | collective-permute-done | bytes 151584 | tf_op jit(solution)/shard_map/ppermute | solution.py:209
  41.4 0.5 collective-permute-start.25
  41.9 0.1 collective-permute-start.31
  42.0 0.4 collective-permute-start.27
  42.4 1.0 %copy-done = f32[64,2048]{1,0:T(8,128)S(1)} copy-done((f32[64,2048]{1,0:T(8,128)S(1)}, f32[64,2048]{1,0:T(8,128)}, u32[]{:S(2)}) %copy-start) | copy-done | bytes 524312
  43.4 0.4 split.1
  43.9 1.1 %own_product.2.refs_9_ = f32[288,256]{1,0:T(8,128)S(1)} custom-call(bf16[256,2048]{1,0:T(8,128)(2,1)S(1)} %get-tuple-element.156.high_ref, bf16[256,2048]{1,0:T(8,128)(2,1)S(1)} %get-tuple-element.157.low_ref, f32[296,128]{1,0:T(8,128)S(1)} %get-tuple-element.68.refs_0_, f32[296,128]{1,0:T(8,128)S(1)} %collective-permute-done.20.refs_1_, ...), custom_call_target="tpu_custom_call" | custom-call | tf_op jit(solution)/shard_map/own_product/pallas_call | solution.py:262
  45.0 1.9 %product.2 = f32[16,40,128]{2,1,0:T(8,128)} custom-call(bf16[256,2048]{1,0:T(8,128)(2,1)S(1)} %get-tuple-element.156.high_ref, bf16[256,2048]{1,0:T(8,128)(2,1)S(1)} %get-tuple-element.157.low_ref, f32[296,128]{1,0:T(8,128)S(1)} %collective-permute-done.19.refs_0_, f32[296,128]{1,0:T(8,128)S(1)} %collective-permute-done.21.refs_1_, ...), custom_call_target="tpu_custom_call" | custom-call | tf_op jit(solution)/shard_map/product/pallas_call | solution.py:271
  46.9 5.0 %all-to-all-start.1 = ((f32[16,40,128]{2,1,0:T(8,128)}), f32[16,40,128]{2,1,0:T(8,128)S(1)}, u32[]{:S(2)}, u32[]{:S(2)}) async-start(f32[16,40,128]{2,1,0:T(8,128)} %product.2), calls=%async_computation.1 | async-start | bytes 655360 | tf_op jit(solution)/shard_map/all_to_all | solution.py:280
  51.9 8.3 %all-to-all-done.1.parts_ref = f32[16,40,128]{2,1,0:T(8,128)S(1)} async-done(((f32[16,40,128]{2,1,0:T(8,128)}), f32[16,40,128]{2,1,0:T(8,128)S(1)}, u32[]{:S(2)}, u32[]{:S(2)}) %all-to-all-start.1) | async-done | bytes 327712 | tf_op jit(solution)/shard_map/all_to_all | solution.py:280
  60.2 0.3 expand.2
  60.5 0.6 while.10
  61.1 0.0 copy-start.3
  61.1 0.6 %copy-done.3 = f32[64,384]{1,0:T(8,128)} copy-done((f32[64,384]{1,0:T(8,128)}, f32[64,384]{1,0:T(8,128)S(1)}, u32[]{:S(2)}) %copy-start.3) | copy-done | bytes 98328
  (29 shorter events, 0.1 us)
Async XLA Ops:
  0.0 7.0 %copy-start.4 = (s32[1536]{0:T(1024)S(1)}, s32[1536]{0:T(1024)}, u32[]{:S(2)}) copy-start(s32[1536]{0:T(1024)} %param.11) | copy-start | bytes 18436
  0.0 7.0 %copy-start.5 = (s32[128]{0:T(128)S(1)}, s32[128]{0:T(128)}, u32[]{:S(2)}) copy-start(s32[128]{0:T(128)} %param.10) | copy-start | bytes 1540
  0.0 7.0 %copy-start.1 = (f32[128,1536]{1,0:T(8,128)S(1)}, f32[128,1536]{1,0:T(8,128)}, u32[]{:S(2)}) copy-start(f32[128,1536]{1,0:T(8,128)} %integrals_ref.1) | copy-start | bytes 2359300
  0.0 43.8 %copy-start.2 = (s32[4096]{0:T(1024)S(1)}, s32[4096]{0:T(1024)}, u32[]{:S(2)}) copy-start(s32[4096]{0:T(1024)} %param.9) | copy-start | bytes 49156
  3.7 20.8 %collective-permute-start.15 = (f32[64,3072]{1,0:T(8,128)}, f32[64,3072]{1,0:T(8,128)S(1)}, u32[]{:S(2)}, u32[]{:S(2)}) collective-permute-start(f32[64,3072]{1,0:T(8,128)} %get-tuple-element.64), channel_id=1, source_target_pairs={{0,8},{8,16},{16,24},{24,0},{1,9},{9,17},{17,25},{25,1},{2,10},{10... | collective-permute-start | bytes 2359304 | tf_op jit(solution)/shard_map/ppermute | solution.py:209
  5.3 25.1 %collective-permute-start.16 = (f32[64,3072]{1,0:T(8,128)}, f32[64,3072]{1,0:T(8,128)S(1)}, u32[]{:S(2)}, u32[]{:S(2)}) collective-permute-start(f32[64,3072]{1,0:T(8,128)} %get-tuple-element.65), channel_id=1, source_target_pairs={{0,24},{8,0},{16,8},{24,16},{1,25},{9,1},{17,9},{25,17},{2,26},{10... | collective-permute-start | bytes 2359304 | tf_op jit(solution)/shard_map/ppermute | solution.py:209
  7.9 8.7 %collective-permute-start.20 = (f32[296,128]{1,0:T(8,128)S(1)}, f32[296,128]{1,0:T(8,128)S(1)}, u32[]{:S(2)}, u32[]{:S(2)}) collective-permute-start(f32[296,128]{1,0:T(8,128)S(1)} %get-tuple-element.68.refs_0_), channel_id=1, source_target_pairs={{0,224},{32,0},{64,32},{96,64},{128,96},{160,128},{192,160},{224,1... | collective-permute-start | bytes 454664 | tf_op jit(solution)/shard_map/ppermute | solution.py:209
  13.8 6.5 %collective-permute-start.28 = (f32[296,128]{1,0:T(8,128)S(1)}, f32[296,128]{1,0:T(8,128)S(1)}, u32[]{:S(2)}, u32[]{:S(2)}) collective-permute-start(f32[296,128]{1,0:T(8,128)S(1)} %get-tuple-element.68.refs_0_), channel_id=1, source_target_pairs={{0,32},{32,64},{64,96},{96,128},{128,160},{160,192},{192,224},{224... | collective-permute-start | bytes 454664 | tf_op jit(solution)/shard_map/ppermute | solution.py:209
  16.6 6.4 %collective-permute-start.22 = (f32[296,128]{1,0:T(8,128)S(1)}, f32[296,128]{1,0:T(8,128)S(1)}, u32[]{:S(2)}, u32[]{:S(2)}) collective-permute-start(f32[296,128]{1,0:T(8,128)S(1)} %collective-permute-done.20.refs_1_), channel_id=1, source_target_pairs={{0,224},{32,0},{64,32},{96,64},{128,96},{160,128},{192,160},{224,1... | collective-permute-start | bytes 454664 | tf_op jit(solution)/shard_map/ppermute | solution.py:209
  20.3 10.6 %collective-permute-start.19 = (f32[296,128]{1,0:T(8,128)S(1)}, f32[296,128]{1,0:T(8,128)S(1)}, u32[]{:S(2)}, u32[]{:S(2)}) collective-permute-start(f32[296,128]{1,0:T(8,128)S(1)} %get-tuple-element.68.refs_0_), channel_id=1, source_target_pairs={{0,4},{4,0},{1,5},{5,1},{2,6},{6,2},{3,7},{7,3},{8,12},{12,8},{9,1... | collective-permute-start | bytes 454664 | tf_op jit(solution)/shard_map/ppermute | solution.py:209
  20.3 13.5 %collective-permute-start.29 = (f32[296,128]{1,0:T(8,128)S(1)}, f32[296,128]{1,0:T(8,128)S(1)}, u32[]{:S(2)}, u32[]{:S(2)}) collective-permute-start(f32[296,128]{1,0:T(8,128)S(1)} %collective-permute-done.28.refs_7_), channel_id=1, source_target_pairs={{0,32},{32,64},{64,96},{96,128},{128,160},{160,192},{192,224},{224... | collective-permute-start | bytes 454664 | tf_op jit(solution)/shard_map/ppermute | solution.py:209
  23.0 10.8 %collective-permute-start.21 = (f32[296,128]{1,0:T(8,128)S(1)}, f32[296,128]{1,0:T(8,128)S(1)}, u32[]{:S(2)}, u32[]{:S(2)}) collective-permute-start(f32[296,128]{1,0:T(8,128)S(1)} %collective-permute-done.20.refs_1_), channel_id=1, source_target_pairs={{0,4},{4,0},{1,5},{5,1},{2,6},{6,2},{3,7},{7,3},{8,12},{12,8},{9,1... | collective-permute-start | bytes 454664 | tf_op jit(solution)/shard_map/ppermute | solution.py:209
  24.5 9.3 %collective-permute-start.24 = (f32[296,128]{1,0:T(8,128)S(1)}, f32[296,128]{1,0:T(8,128)S(1)}, u32[]{:S(2)}, u32[]{:S(2)}) collective-permute-start(f32[296,128]{1,0:T(8,128)S(1)} %collective-permute-done.22.refs_2_), channel_id=1, source_target_pairs={{0,224},{32,0},{64,32},{96,64},{128,96},{160,128},{192,160},{224,1... | collective-permute-start | bytes 454664 | tf_op jit(solution)/shard_map/ppermute | solution.py:209
  30.4 11.4 %collective-permute-start.17 = (f32[64,1024]{1,0:T(8,128)S(1)}, f32[64,1024]{1,0:T(8,128)S(1)}, u32[]{:S(2)}, u32[]{:S(2)}) collective-permute-start(f32[64,1024]{1,0:T(8,128)S(1)} %slice.8), channel_id=1, source_target_pairs={{0,8},{8,16},{16,24},{24,0},{1,9},{9,17},{17,25},{25,1},{2,10},{10... | collective-permute-start | bytes 786440 | tf_op jit(solution)/shard_map/ppermute | solution.py:209
  30.8 11.1 %collective-permute-start.18 = (f32[64,1024]{1,0:T(8,128)S(1)}, f32[64,1024]{1,0:T(8,128)S(1)}, u32[]{:S(2)}, u32[]{:S(2)}) collective-permute-start(f32[64,1024]{1,0:T(8,128)S(1)} %slice.9), channel_id=1, source_target_pairs={{0,24},{8,0},{16,8},{24,16},{1,25},{9,1},{17,9},{25,17},{2,26},{10... | collective-permute-start | bytes 786440 | tf_op jit(solution)/shard_map/ppermute | solution.py:209
  33.8 3.3 %collective-permute-start.33 = (f32[296,128]{1,0:T(8,128)S(1)}, f32[296,128]{1,0:T(8,128)S(1)}, u32[]{:S(2)}, u32[]{:S(2)}) collective-permute-start(f32[296,128]{1,0:T(8,128)S(1)} %collective-permute-done.28.refs_7_), channel_id=1, source_target_pairs={{0,4},{4,0},{1,5},{5,1},{2,6},{6,2},{3,7},{7,3},{8,12},{12,8},{9,1... | collective-permute-start | bytes 454664 | tf_op jit(solution)/shard_map/ppermute | solution.py:209
  33.8 7.6 %collective-permute-start.30 = (f32[296,128]{1,0:T(8,128)S(1)}, f32[296,128]{1,0:T(8,128)S(1)}, u32[]{:S(2)}, u32[]{:S(2)}) collective-permute-start(f32[296,128]{1,0:T(8,128)S(1)} %collective-permute-done.29.refs_6_), channel_id=1, source_target_pairs={{0,32},{32,64},{64,96},{96,128},{128,160},{160,192},{192,224},{224... | collective-permute-start | bytes 454664 | tf_op jit(solution)/shard_map/ppermute | solution.py:209
  33.9 7.5 %collective-permute-start.26 = (f32[296,128]{1,0:T(8,128)S(1)}, f32[296,128]{1,0:T(8,128)S(1)}, u32[]{:S(2)}, u32[]{:S(2)}) collective-permute-start(f32[296,128]{1,0:T(8,128)S(1)} %collective-permute-done.24.refs_3_), channel_id=1, source_target_pairs={{0,224},{32,0},{64,32},{96,64},{128,96},{160,128},{192,160},{224,1... | collective-permute-start | bytes 454664 | tf_op jit(solution)/shard_map/ppermute | solution.py:209
  37.1 7.9 %collective-permute-start.23 = (f32[296,128]{1,0:T(8,128)S(1)}, f32[296,128]{1,0:T(8,128)S(1)}, u32[]{:S(2)}, u32[]{:S(2)}) collective-permute-start(f32[296,128]{1,0:T(8,128)S(1)} %collective-permute-done.22.refs_2_), channel_id=1, source_target_pairs={{0,4},{4,0},{1,5},{5,1},{2,6},{6,2},{3,7},{7,3},{8,12},{12,8},{9,1... | collective-permute-start | bytes 454664 | tf_op jit(solution)/shard_map/ppermute | solution.py:209
  41.4 3.6 %collective-permute-start.32 = (f32[296,128]{1,0:T(8,128)S(1)}, f32[296,128]{1,0:T(8,128)S(1)}, u32[]{:S(2)}, u32[]{:S(2)}) collective-permute-start(f32[296,128]{1,0:T(8,128)S(1)} %collective-permute-done.29.refs_6_), channel_id=1, source_target_pairs={{0,4},{4,0},{1,5},{5,1},{2,6},{6,2},{3,7},{7,3},{8,12},{12,8},{9,1... | collective-permute-start | bytes 454664 | tf_op jit(solution)/shard_map/ppermute | solution.py:209
  41.4 3.6 %collective-permute-start.25 = (f32[296,128]{1,0:T(8,128)S(1)}, f32[296,128]{1,0:T(8,128)S(1)}, u32[]{:S(2)}, u32[]{:S(2)}) collective-permute-start(f32[296,128]{1,0:T(8,128)S(1)} %collective-permute-done.24.refs_3_), channel_id=1, source_target_pairs={{0,4},{4,0},{1,5},{5,1},{2,6},{6,2},{3,7},{7,3},{8,12},{12,8},{9,1... | collective-permute-start | bytes 454664 | tf_op jit(solution)/shard_map/ppermute | solution.py:209
  41.9 3.1 %collective-permute-start.31 = (f32[296,128]{1,0:T(8,128)S(1)}, f32[296,128]{1,0:T(8,128)S(1)}, u32[]{:S(2)}, u32[]{:S(2)}) collective-permute-start(f32[296,128]{1,0:T(8,128)S(1)} %collective-permute-done.30.refs_5_), channel_id=1, source_target_pairs={{0,4},{4,0},{1,5},{5,1},{2,6},{6,2},{3,7},{7,3},{8,12},{12,8},{9,1... | collective-permute-start | bytes 454664 | tf_op jit(solution)/shard_map/ppermute | solution.py:209
  42.0 3.0 %collective-permute-start.27 = (f32[296,128]{1,0:T(8,128)S(1)}, f32[296,128]{1,0:T(8,128)S(1)}, u32[]{:S(2)}, u32[]{:S(2)}) collective-permute-start(f32[296,128]{1,0:T(8,128)S(1)} %collective-permute-done.26.refs_4_), channel_id=1, source_target_pairs={{0,4},{4,0},{1,5},{5,1},{2,6},{6,2},{3,7},{7,3},{8,12},{12,8},{9,1... | collective-permute-start | bytes 454664 | tf_op jit(solution)/shard_map/ppermute | solution.py:209
  42.4 1.0 %copy-start = (f32[64,2048]{1,0:T(8,128)S(1)}, f32[64,2048]{1,0:T(8,128)}, u32[]{:S(2)}) copy-start(f32[64,2048]{1,0:T(8,128)} %get-tuple-element.63.own_ref) | copy-start | bytes 1572868
  46.9 13.3 %all-to-all-start.1 = ((f32[16,40,128]{2,1,0:T(8,128)}), f32[16,40,128]{2,1,0:T(8,128)S(1)}, u32[]{:S(2)}, u32[]{:S(2)}) async-start(f32[16,40,128]{2,1,0:T(8,128)} %product.2), calls=%async_computation.1 | async-start | bytes 655360 | tf_op jit(solution)/shard_map/all_to_all | solution.py:280
  61.1 0.6 %copy-start.3 = (f32[64,384]{1,0:T(8,128)}, f32[64,384]{1,0:T(8,128)S(1)}, u32[]{:S(2)}) copy-start(f32[64,384]{1,0:T(8,128)S(1)} %get-tuple-element.246) | copy-start | bytes 294916

commit v4 on v3

--- a/solution.py
+++ b/solution.py
@@ -122,19 +122,18 @@
     compact(round_ref[0] * SLOTS, integrals_ref, pair_ref, slab_ref, rank_ref, out_ref)
 
 
-def split_kernel(own_ref, up_ref, down_ref, far_up_ref, far_down_ref, high_ref, low_ref, own, sem):
-    copy = pltpu.make_async_copy(own_ref, own, sem)
-    copy.start()
+def own_split_kernel(own_ref, high_ref, low_ref):
+    high_ref[...], low_ref[...] = split(own_ref[...])
+
+
+def split_kernel(up_ref, down_ref, far_up_ref, far_down_ref, high_ref, low_ref):
     half = AB_GROUP // 2
-    for d, ref in ((1, up_ref), (2, down_ref)):
+    for d, ref in enumerate((up_ref, down_ref)):
         row = pl.ds(d * ROW_DEV, ROW_DEV)
         high_ref[row, :], low_ref[row, :] = split(ref[:, :AB_GROUP])
-    row = pl.ds(3 * ROW_DEV, ROW_DEV)
+    row = pl.ds(2 * ROW_DEV, ROW_DEV)
     high_ref[row, :half], low_ref[row, :half] = split(far_up_ref[...])
     high_ref[row, half:], low_ref[row, half:] = split(far_down_ref[...])
-    copy.wait()
-    row = pl.ds(0, ROW_DEV)
-    high_ref[row, :], low_ref[row, :] = split(own[...])
 
 
 def row_labels(rows_ref, z, y, c):
@@ -142,7 +141,7 @@
     return jnp.where(c == 0, both[:ROW_DEV], both[ROW_DEV:])
 
 
-def masked_product(high_ref, low_ref, blocks, other, rows_ref, thigh, tlow, vhigh, vlow):
+def masked_product(halves, blocks, other, rows_ref, thigh, tlow, vhigh, vlow):
     z, y, c, x = place()
     core = lax.rem(c + other, C)
     columns = []
@@ -153,29 +152,33 @@
     for d, shift in enumerate(SHIFTS):
         labels = row_labels(rows_ref, z, lax.rem(y - shift + Y, Y), c)
         rows = pl.ds(d * ROW_DEV, ROW_DEV)
+        high_ref, low_ref = halves[:2] if d == 0 else halves[2:]
+        source = pl.ds(max(d - 1, 0) * ROW_DEV, ROW_DEV)
         for k in range(Z):
             at = pl.ds(pl.multiple_of((lax.rem(z + k, Z) * C + core) * AB_DEV, AB_DEV), AB_DEV)
             to = pl.ds(k * AB_DEV, AB_DEV)
             mask = jnp.where(labels == columns[k], 1.0, 0.0).astype(jnp.bfloat16)
-            thigh[rows, to] = high_ref[rows, at] * mask
-            tlow[rows, to] = low_ref[rows, at] * mask
+            thigh[rows, to] = high_ref[source, at] * mask
+            tlow[rows, to] = low_ref[source, at] * mask
     total = lax.dot_general(vhigh[...], thigh[...], NT, preferred_element_type=jnp.float32)
     total += lax.dot_general(vlow[...], thigh[...], NT, preferred_element_type=jnp.float32)
     total += lax.dot_general(vhigh[...], tlow[...], NT, preferred_element_type=jnp.float32)
     return total
 
 
-def own_product_kernel(high_ref, low_ref, *refs):
+def own_product_kernel(*refs):
+    halves, refs = refs[:4], refs[4:]
     blocks = refs[:Z]
     rows_ref, out_ref, *scratch = refs[Z:]
-    out_ref[...] = masked_product(high_ref, low_ref, blocks, 0, rows_ref, *scratch)
-
-
-def product_kernel(high_ref, low_ref, *refs):
+    out_ref[...] = masked_product(halves, blocks, 0, rows_ref, *scratch)
+
+
+def product_kernel(*refs):
+    halves, refs = refs[:4], refs[4:]
     blocks = refs[:Z]
     rows_ref, sum_ref, out_ref, *scratch = refs[Z:]
     z, y, c, x = place()
-    total = sum_ref[...] + masked_product(high_ref, low_ref, blocks, 1, rows_ref, *scratch)
+    total = sum_ref[...] + masked_product(halves, blocks, 1, rows_ref, *scratch)
     for d, shift in enumerate(SHIFTS):
         target = lax.rem(y - shift + Y, Y)
         for q in range(X):
@@ -262,7 +265,7 @@
         partial = pl.pallas_call(
             own_product_kernel,
             out_shape=f32(LABEL, Y * ROW_DEV),
-            in_specs=[VMEM] * (2 + Z + 1),
+            in_specs=[VMEM] * (4 + Z + 1),
             out_specs=VMEM,
             scratch_shapes=scratch,
             compiler_params=PARAMS,
@@ -271,7 +274,7 @@
         parts = pl.pallas_call(
             product_kernel,
             out_shape=f32(Y * X, FOLD, 2 * ROW_DEV),
-            in_specs=[VMEM] * (4 + Z),
+            in_specs=[VMEM] * (6 + Z),
             out_specs=VMEM,
             scratch_shapes=scratch,
             compiler_params=PARAMS,
@@ -294,19 +297,28 @@
 
     number = jnp.zeros((), jnp.int32)
     packed, rank, rounds = pack(number)
+    own_halves = pl.pallas_call(
+        own_split_kernel,
+        out_shape=[jax.ShapeDtypeStruct((ROW_DEV, AB_GROUP), jnp.bfloat16)] * 2,
+        in_specs=[VMEM],
+        out_specs=[VMEM] * 2,
+        compiler_params=PARAMS,
+        name="own_split",
+    )(own)
+    own_halves, packed = lax.optimization_barrier((list(own_halves), packed))
     blocks = gather(packed)
     near = [shifted(piece, "y", shift) for piece, shift in zip(pieces, (1, -1))]
     forward = near
     far = [shifted(piece[:, AB_GROUP:], "y", shift) for piece, shift in zip(forward, (1, -1))]
     halves = pl.pallas_call(
         split_kernel,
-        out_shape=[jax.ShapeDtypeStruct((Y * ROW_DEV, AB_GROUP), jnp.bfloat16)] * 2,
-        in_specs=[ANY] + [VMEM] * 4,
+        out_shape=[jax.ShapeDtypeStruct((3 * ROW_DEV, AB_GROUP), jnp.bfloat16)] * 2,
+        in_specs=[VMEM] * 4,
         out_specs=[VMEM] * 2,
-        scratch_shapes=[pltpu.VMEM((ROW_DEV, AB_GROUP), jnp.float32), pltpu.SemaphoreType.DMA],
         compiler_params=PARAMS,
         name="split",
-    )(own, *near, *far)
+    )(*near, *far)
+    halves = [*own_halves, *halves]
 
 
     first = ladder_round(number, blocks, rank)

time: 62.8 us -> 61.7 us (0.982)
  waiting for transfers between devices: 19.6 us -> 17.9 us
    ppermute x19, waiting for transfers between devices: 11.3 us -> 9.65 us  [shifted(): lax.ppermute(value, axis, [(i, (i + by) % size) for i in range(size)])]
where the time goes in v4:
time: 61.7 us; the launch traced here: 60.6 us
  starting transfers between devices  31.9 us (52%)
  waiting for transfers between devices  17.9 us (29%)
  Pallas kernels  8.14 us (13%)
  local copies, waits for them, and re-layouts  1.73 us (3%)
  loops' own time  0.7 us (1%)
    ppermute x19, starting transfers between devices, shifted(): lax.ppermute(value, axis, [(i, (i + by) % size) for i in range(size)])  26.9 us
    ppermute x19, waiting for transfers between devices, shifted(): lax.ppermute(value, axis, [(i, (i + by) % size) for i in range(size)])  9.65 us
    all_to_all x1, waiting for transfers between devices, ladder_round(): lax.all_to_all(parts, ('y', 'x'), split_axis=0, concat_axis=0, tiled=True)  8.28 us
    all_to_all x1, starting transfers between devices, ladder_round(): lax.all_to_all(parts, ('y', 'x'), split_axis=0, concat_axis=0, tiled=True)  4.99 us
    pallas_call x1, Pallas kernels, per_device(): pl.pallas_call(select_kernel, out_shape=[f32(ROW_DEV, AB_GROUP * 3 // 2)]...  3.64 us
    pallas_call x1, Pallas kernels, ladder_round(): pl.pallas_call(product_kernel, out_shape=f32(Y * X, FOLD, 2 * ROW_DEV), i...  1.9 us
    unnamed x12, local copies, waits for them, and re-layouts  1.69 us
  transfers between devices with their start and end apart: 20, of which 5 were waited for; matrix products, arithmetic and copies ran while one was open for 0% of the time, Pallas kernels for 4%

profile of v4, /device:TPU:2, one launch (start us, length us, event | category | flops | bytes accessed | tf_op | source)
XLA Modules:
  0.0 60.6 jit_solution(17397947149332171350)
XLA Ops:
  0.0 3.6 %select.1 = (f32[64,3072]{1,0:T(8,128)}, f32[64,3072]{1,0:T(8,128)}, f32[64,2048]{1,0:T(8,128)}) custom-call(f32[64,32768]{1,0:T(8,128)} %amplitudes_ref.1), custom_call_target="tpu_custom_call" | custom-call | tf_op jit(solution)/shard_map/select/pallas_call | solution.py:227
  3.7 1.7 %collective-permute-start.15 = (f32[64,3072]{1,0:T(8,128)}, f32[64,3072]{1,0:T(8,128)S(1)}, u32[]{:S(2)}, u32[]{:S(2)}) collective-permute-start(f32[64,3072]{1,0:T(8,128)} %get-tuple-element.84), channel_id=1, source_target_pairs={{0,8},{8,16},{16,24},{24,0},{1,9},{9,17},{17,25},{25,1},{2,10},{10... | collective-permute-start | bytes 2359304 | tf_op jit(solution)/shard_map/ppermute | solution.py:212
  5.3 1.7 %collective-permute-start.16 = (f32[64,3072]{1,0:T(8,128)}, f32[64,3072]{1,0:T(8,128)S(1)}, u32[]{:S(2)}, u32[]{:S(2)}) collective-permute-start(f32[64,3072]{1,0:T(8,128)} %get-tuple-element.85), channel_id=1, source_target_pairs={{0,24},{8,0},{16,8},{24,16},{1,25},{9,1},{17,9},{25,17},{2,26},{10... | collective-permute-start | bytes 2359304 | tf_op jit(solution)/shard_map/ppermute | solution.py:212
  7.0 1.0 %copy-done = f32[64,2048]{1,0:T(8,128)S(1)} copy-done((f32[64,2048]{1,0:T(8,128)S(1)}, f32[64,2048]{1,0:T(8,128)}, u32[]{:S(2)}) %copy-start) | copy-done | bytes 524312
  8.0 0.1 own_split.1
  8.2 0.8 %compact.2 = (f32[296,128]{1,0:T(8,128)S(1)}, s32[12,128]{1,0:T(8,128)S(1)}, s32[1]{0:T(128)}) custom-call(s32[1]{0:T(128)} %constant.2.clone.1.round_ref, f32[128,1536]{1,0:T(8,128)S(1)} %copy-done.1, s32[1,128]{1,0:T(1,128)S(1)} %bitcast.15, s32[12,128]{1,0:T(8,128)S(1)} %bitcast.12), custom_call_target="tpu_custom_call" | custom-call | tf_op jit(solution)/shard_map/compact/pallas_call | solution.py:237
  9.0 5.9 %collective-permute-start.20 = (f32[296,128]{1,0:T(8,128)S(1)}, f32[296,128]{1,0:T(8,128)S(1)}, u32[]{:S(2)}, u32[]{:S(2)}) collective-permute-start(f32[296,128]{1,0:T(8,128)S(1)} %get-tuple-element.88.refs_4_), channel_id=1, source_target_pairs={{0,224},{32,0},{64,32},{96,64},{128,96},{160,128},{192,160},{224,1... | collective-permute-start | bytes 454664 | tf_op jit(solution)/shard_map/ppermute | solution.py:212
  14.9 2.8 %collective-permute-done.20.refs_5_ = f32[296,128]{1,0:T(8,128)S(1)} collective-permute-done((f32[296,128]{1,0:T(8,128)S(1)}, f32[296,128]{1,0:T(8,128)S(1)}, u32[]{:S(2)}, u32[]{:S(2)}) %collective-permute-start.20) | collective-permute-done | bytes 151584 | tf_op jit(solution)/shard_map/ppermute | solution.py:212
  17.7 3.7 %collective-permute-start.22 = (f32[296,128]{1,0:T(8,128)S(1)}, f32[296,128]{1,0:T(8,128)S(1)}, u32[]{:S(2)}, u32[]{:S(2)}) collective-permute-start(f32[296,128]{1,0:T(8,128)S(1)} %collective-permute-done.20.refs_5_), channel_id=1, source_target_pairs={{0,224},{32,0},{64,32},{96,64},{128,96},{160,128},{192,160},{224,1... | collective-permute-start | bytes 454664 | tf_op jit(solution)/shard_map/ppermute | solution.py:212
  21.4 0.5 collective-permute-start.21
  21.9 2.2 %collective-permute-done.22.refs_6_ = f32[296,128]{1,0:T(8,128)S(1)} collective-permute-done((f32[296,128]{1,0:T(8,128)S(1)}, f32[296,128]{1,0:T(8,128)S(1)}, u32[]{:S(2)}, u32[]{:S(2)}) %collective-permute-start.22) | collective-permute-done | bytes 151584 | tf_op jit(solution)/shard_map/ppermute | solution.py:212
  24.1 0.0 collective-permute-start.29
  24.1 0.4 collective-permute-done.15.up_ref
  24.5 5.9 %collective-permute-start.24 = (f32[296,128]{1,0:T(8,128)S(1)}, f32[296,128]{1,0:T(8,128)S(1)}, u32[]{:S(2)}, u32[]{:S(2)}) collective-permute-start(f32[296,128]{1,0:T(8,128)S(1)} %collective-permute-done.22.refs_6_), channel_id=1, source_target_pairs={{0,224},{32,0},{64,32},{96,64},{128,96},{160,128},{192,160},{224,1... | collective-permute-start | bytes 454664 | tf_op jit(solution)/shard_map/ppermute | solution.py:212
  30.4 0.4 collective-permute-start.17
  30.8 2.9 %collective-permute-start.18 = (f32[64,1024]{1,0:T(8,128)S(1)}, f32[64,1024]{1,0:T(8,128)S(1)}, u32[]{:S(2)}, u32[]{:S(2)}) collective-permute-start(f32[64,1024]{1,0:T(8,128)S(1)} %slice.9), channel_id=1, source_target_pairs={{0,24},{8,0},{16,8},{24,16},{1,25},{9,1},{17,9},{25,17},{2,26},{10... | collective-permute-start | bytes 786440 | tf_op jit(solution)/shard_map/ppermute | solution.py:212
  33.8 0.1 collective-permute-start.30
  33.9 3.2 %collective-permute-start.26 = (f32[296,128]{1,0:T(8,128)S(1)}, f32[296,128]{1,0:T(8,128)S(1)}, u32[]{:S(2)}, u32[]{:S(2)}) collective-permute-start(f32[296,128]{1,0:T(8,128)S(1)} %collective-permute-done.24.refs_7_), channel_id=1, source_target_pairs={{0,224},{32,0},{64,32},{96,64},{128,96},{160,128},{192,160},{224,1... | collective-permute-start | bytes 454664 | tf_op jit(solution)/shard_map/ppermute | solution.py:212
  37.1 4.2 %collective-permute-done.30.refs_9_ = f32[296,128]{1,0:T(8,128)S(1)} collective-permute-done((f32[296,128]{1,0:T(8,128)S(1)}, f32[296,128]{1,0:T(8,128)S(1)}, u32[]{:S(2)}, u32[]{:S(2)}) %collective-permute-start.30) | collective-permute-done | bytes 151584 | tf_op jit(solution)/shard_map/ppermute | solution.py:212
  41.3 0.0 collective-permute-start.32
  41.3 0.5 collective-permute-start.25
  41.9 0.1 collective-permute-start.31
  41.9 0.4 collective-permute-start.27
  42.4 0.3 split.1
  42.6 1.1 %own_product.2.refs_13_ = f32[288,256]{1,0:T(8,128)S(1)} custom-call(bf16[64,2048]{1,0:T(8,128)(2,1)S(1)} %get-tuple-element.192.refs_0_, bf16[64,2048]{1,0:T(8,128)(2,1)S(1)} %get-tuple-element.193.refs_1_, bf16[192,2048]{1,0:T(8,128)(2,1)S(1)} %get-tuple-element.194.refs_2_, bf16[192,2048]{1,0:T(8,128)(2,1)S(1)} %get-tuple-element.195.refs_3_, ...), custom_call_target="tpu_custom_call" | custom-call | tf_op jit(solution)/shard_map/own_product/pallas_call | solution.py:265
  43.8 1.9 %product.2 = f32[16,40,128]{2,1,0:T(8,128)} custom-call(bf16[64,2048]{1,0:T(8,128)(2,1)S(1)} %get-tuple-element.192.refs_0_, bf16[64,2048]{1,0:T(8,128)(2,1)S(1)} %get-tuple-element.193.refs_1_, bf16[192,2048]{1,0:T(8,128)(2,1)S(1)} %get-tuple-element.194.refs_2_, bf16[192,2048]{1,0:T(8,128)(2,1)S(1)} %get-tuple-element.195.refs_3_, ...), custom_call_target="tpu_custom_call" | custom-call | tf_op jit(solution)/shard_map/product/pallas_call | solution.py:274
  45.7 5.0 %all-to-all-start.1 = ((f32[16,40,128]{2,1,0:T(8,128)}), f32[16,40,128]{2,1,0:T(8,128)S(1)}, u32[]{:S(2)}, u32[]{:S(2)}) async-start(f32[16,40,128]{2,1,0:T(8,128)} %product.2), calls=%async_computation.1 | async-start | bytes 655360 | tf_op jit(solution)/shard_map/all_to_all | solution.py:283
  50.7 8.3 %all-to-all-done.1.parts_ref = f32[16,40,128]{2,1,0:T(8,128)S(1)} async-done(((f32[16,40,128]{2,1,0:T(8,128)}), f32[16,40,128]{2,1,0:T(8,128)S(1)}, u32[]{:S(2)}, u32[]{:S(2)}) %all-to-all-start.1) | async-done | bytes 327712 | tf_op jit(solution)/shard_map/all_to_all | solution.py:283
  59.0 0.3 expand.2
  59.3 0.7 %while.10 = (s32[]{:T(128)}, f32[64,384]{1,0:T(8,128)S(1)}, s32[1]{0:T(128)}, f32[128,1536]{1,0:T(8,128)S(1)}, s32[1,128]{1,0:T(1,128)S(1)}, /*index=5*/s32[12,1...) while((s32[]{:T(128)}, f32[64,384]{1,0:T(8,128)S(1)}, ...), condition=%wide.region_1.0_spmd, body=%wide.region_0.0_spmd.sunk | while | flops 24578 | bytes 10371829 | solution.py:325
  60.0 0.0 copy-start.3
  60.0 0.6 %copy-done.3 = f32[64,384]{1,0:T(8,128)} copy-done((f32[64,384]{1,0:T(8,128)}, f32[64,384]{1,0:T(8,128)S(1)}, u32[]{:S(2)}) %copy-start.3) | copy-done | bytes 98328
  (30 shorter events, 0.1 us)
Async XLA Ops:
  0.0 8.1 %copy-start.1 = (f32[128,1536]{1,0:T(8,128)S(1)}, f32[128,1536]{1,0:T(8,128)}, u32[]{:S(2)}) copy-start(f32[128,1536]{1,0:T(8,128)} %integrals_ref.1) | copy-start | bytes 2359300
  0.0 8.1 %copy-start.5 = (s32[128]{0:T(128)S(1)}, s32[128]{0:T(128)}, u32[]{:S(2)}) copy-start(s32[128]{0:T(128)} %param.10) | copy-start | bytes 1540
  0.0 8.1 %copy-start.4 = (s32[1536]{0:T(1024)S(1)}, s32[1536]{0:T(1024)}, u32[]{:S(2)}) copy-start(s32[1536]{0:T(1024)} %param.11) | copy-start | bytes 18436
  0.0 42.6 %copy-start.2 = (s32[4096]{0:T(1024)S(1)}, s32[4096]{0:T(1024)}, u32[]{:S(2)}) copy-start(s32[4096]{0:T(1024)} %param.9) | copy-start | bytes 49156
  3.7 20.8 %collective-permute-start.15 = (f32[64,3072]{1,0:T(8,128)}, f32[64,3072]{1,0:T(8,128)S(1)}, u32[]{:S(2)}, u32[]{:S(2)}) collective-permute-start(f32[64,3072]{1,0:T(8,128)} %get-tuple-element.84), channel_id=1, source_target_pairs={{0,8},{8,16},{16,24},{24,0},{1,9},{9,17},{17,25},{25,1},{2,10},{10... | collective-permute-start | bytes 2359304 | tf_op jit(solution)/shard_map/ppermute | solution.py:212
  5.3 25.1 %collective-permute-start.16 = (f32[64,3072]{1,0:T(8,128)}, f32[64,3072]{1,0:T(8,128)S(1)}, u32[]{:S(2)}, u32[]{:S(2)}) collective-permute-start(f32[64,3072]{1,0:T(8,128)} %get-tuple-element.85), channel_id=1, source_target_pairs={{0,24},{8,0},{16,8},{24,16},{1,25},{9,1},{17,9},{25,17},{2,26},{10... | collective-permute-start | bytes 2359304 | tf_op jit(solution)/shard_map/ppermute | solution.py:212
  7.0 1.0 %copy-start = (f32[64,2048]{1,0:T(8,128)S(1)}, f32[64,2048]{1,0:T(8,128)}, u32[]{:S(2)}) copy-start(f32[64,2048]{1,0:T(8,128)} %get-tuple-element.78.own_ref) | copy-start | bytes 1572868
  9.0 8.7 %collective-permute-start.20 = (f32[296,128]{1,0:T(8,128)S(1)}, f32[296,128]{1,0:T(8,128)S(1)}, u32[]{:S(2)}, u32[]{:S(2)}) collective-permute-start(f32[296,128]{1,0:T(8,128)S(1)} %get-tuple-element.88.refs_4_), channel_id=1, source_target_pairs={{0,224},{32,0},{64,32},{96,64},{128,96},{160,128},{192,160},{224,1... | collective-permute-start | bytes 454664 | tf_op jit(solution)/shard_map/ppermute | solution.py:212
  14.9 6.5 %collective-permute-start.28 = (f32[296,128]{1,0:T(8,128)S(1)}, f32[296,128]{1,0:T(8,128)S(1)}, u32[]{:S(2)}, u32[]{:S(2)}) collective-permute-start(f32[296,128]{1,0:T(8,128)S(1)} %get-tuple-element.88.refs_4_), channel_id=1, source_target_pairs={{0,32},{32,64},{64,96},{96,128},{128,160},{160,192},{192,224},{224... | collective-permute-start | bytes 454664 | tf_op jit(solution)/shard_map/ppermute | solution.py:212
  17.7 6.4 %collective-permute-start.22 = (f32[296,128]{1,0:T(8,128)S(1)}, f32[296,128]{1,0:T(8,128)S(1)}, u32[]{:S(2)}, u32[]{:S(2)}) collective-permute-start(f32[296,128]{1,0:T(8,128)S(1)} %collective-permute-done.20.refs_5_), channel_id=1, source_target_pairs={{0,224},{32,0},{64,32},{96,64},{128,96},{160,128},{192,160},{224,1... | collective-permute-start | bytes 454664 | tf_op jit(solution)/shard_map/ppermute | solution.py:212
  21.4 9.4 %collective-permute-start.19 = (f32[296,128]{1,0:T(8,128)S(1)}, f32[296,128]{1,0:T(8,128)S(1)}, u32[]{:S(2)}, u32[]{:S(2)}) collective-permute-start(f32[296,128]{1,0:T(8,128)S(1)} %get-tuple-element.88.refs_4_), channel_id=1, source_target_pairs={{0,4},{4,0},{1,5},{5,1},{2,6},{6,2},{3,7},{7,3},{8,12},{12,8},{9,1... | collective-permute-start | bytes 454664 | tf_op jit(solution)/shard_map/ppermute | solution.py:212
  21.4 12.3 %collective-permute-start.21 = (f32[296,128]{1,0:T(8,128)S(1)}, f32[296,128]{1,0:T(8,128)S(1)}, u32[]{:S(2)}, u32[]{:S(2)}) collective-permute-start(f32[296,128]{1,0:T(8,128)S(1)} %collective-permute-done.20.refs_5_), channel_id=1, source_target_pairs={{0,4},{4,0},{1,5},{5,1},{2,6},{6,2},{3,7},{7,3},{8,12},{12,8},{9,1... | collective-permute-start | bytes 454664 | tf_op jit(solution)/shard_map/ppermute | solution.py:212
  24.1 9.6 %collective-permute-start.29 = (f32[296,128]{1,0:T(8,128)S(1)}, f32[296,128]{1,0:T(8,128)S(1)}, u32[]{:S(2)}, u32[]{:S(2)}) collective-permute-start(f32[296,128]{1,0:T(8,128)S(1)} %collective-permute-done.28.refs_11_), channel_id=1, source_target_pairs={{0,32},{32,64},{64,96},{96,128},{128,160},{160,192},{192,224},{224... | collective-permute-start | bytes 454664 | tf_op jit(solution)/shard_map/ppermute | solution.py:212
  24.5 9.3 %collective-permute-start.24 = (f32[296,128]{1,0:T(8,128)S(1)}, f32[296,128]{1,0:T(8,128)S(1)}, u32[]{:S(2)}, u32[]{:S(2)}) collective-permute-start(f32[296,128]{1,0:T(8,128)S(1)} %collective-permute-done.22.refs_6_), channel_id=1, source_target_pairs={{0,224},{32,0},{64,32},{96,64},{128,96},{160,128},{192,160},{224,1... | collective-permute-start | bytes 454664 | tf_op jit(solution)/shard_map/ppermute | solution.py:212
  30.4 11.4 %collective-permute-start.17 = (f32[64,1024]{1,0:T(8,128)S(1)}, f32[64,1024]{1,0:T(8,128)S(1)}, u32[]{:S(2)}, u32[]{:S(2)}) collective-permute-start(f32[64,1024]{1,0:T(8,128)S(1)} %slice.8), channel_id=1, source_target_pairs={{0,8},{8,16},{16,24},{24,0},{1,9},{9,17},{17,25},{25,1},{2,10},{10... | collective-permute-start | bytes 786440 | tf_op jit(solution)/shard_map/ppermute | solution.py:212
  30.8 11.1 %collective-permute-start.18 = (f32[64,1024]{1,0:T(8,128)S(1)}, f32[64,1024]{1,0:T(8,128)S(1)}, u32[]{:S(2)}, u32[]{:S(2)}) collective-permute-start(f32[64,1024]{1,0:T(8,128)S(1)} %slice.9), channel_id=1, source_target_pairs={{0,24},{8,0},{16,8},{24,16},{1,25},{9,1},{17,9},{25,17},{2,26},{10... | collective-permute-start | bytes 786440 | tf_op jit(solution)/shard_map/ppermute | solution.py:212
  33.8 3.3 %collective-permute-start.33 = (f32[296,128]{1,0:T(8,128)S(1)}, f32[296,128]{1,0:T(8,128)S(1)}, u32[]{:S(2)}, u32[]{:S(2)}) collective-permute-start(f32[296,128]{1,0:T(8,128)S(1)} %collective-permute-done.28.refs_11_), channel_id=1, source_target_pairs={{0,4},{4,0},{1,5},{5,1},{2,6},{6,2},{3,7},{7,3},{8,12},{12,8},{9,1... | collective-permute-start | bytes 454664 | tf_op jit(solution)/shard_map/ppermute | solution.py:212
  33.8 7.6 %collective-permute-start.30 = (f32[296,128]{1,0:T(8,128)S(1)}, f32[296,128]{1,0:T(8,128)S(1)}, u32[]{:S(2)}, u32[]{:S(2)}) collective-permute-start(f32[296,128]{1,0:T(8,128)S(1)} %collective-permute-done.29.refs_10_), channel_id=1, source_target_pairs={{0,32},{32,64},{64,96},{96,128},{128,160},{160,192},{192,224},{224... | collective-permute-start | bytes 454664 | tf_op jit(solution)/shard_map/ppermute | solution.py:212
  33.9 7.5 %collective-permute-start.26 = (f32[296,128]{1,0:T(8,128)S(1)}, f32[296,128]{1,0:T(8,128)S(1)}, u32[]{:S(2)}, u32[]{:S(2)}) collective-permute-start(f32[296,128]{1,0:T(8,128)S(1)} %collective-permute-done.24.refs_7_), channel_id=1, source_target_pairs={{0,224},{32,0},{64,32},{96,64},{128,96},{160,128},{192,160},{224,1... | collective-permute-start | bytes 454664 | tf_op jit(solution)/shard_map/ppermute | solution.py:212
  37.1 6.7 %collective-permute-start.23 = (f32[296,128]{1,0:T(8,128)S(1)}, f32[296,128]{1,0:T(8,128)S(1)}, u32[]{:S(2)}, u32[]{:S(2)}) collective-permute-start(f32[296,128]{1,0:T(8,128)S(1)} %collective-permute-done.22.refs_6_), channel_id=1, source_target_pairs={{0,4},{4,0},{1,5},{5,1},{2,6},{6,2},{3,7},{7,3},{8,12},{12,8},{9,1... | collective-permute-start | bytes 454664 | tf_op jit(solution)/shard_map/ppermute | solution.py:212
  41.3 2.4 %collective-permute-start.32 = (f32[296,128]{1,0:T(8,128)S(1)}, f32[296,128]{1,0:T(8,128)S(1)}, u32[]{:S(2)}, u32[]{:S(2)}) collective-permute-start(f32[296,128]{1,0:T(8,128)S(1)} %collective-permute-done.29.refs_10_), channel_id=1, source_target_pairs={{0,4},{4,0},{1,5},{5,1},{2,6},{6,2},{3,7},{7,3},{8,12},{12,8},{9,1... | collective-permute-start | bytes 454664 | tf_op jit(solution)/shard_map/ppermute | solution.py:212
  41.3 2.4 %collective-permute-start.25 = (f32[296,128]{1,0:T(8,128)S(1)}, f32[296,128]{1,0:T(8,128)S(1)}, u32[]{:S(2)}, u32[]{:S(2)}) collective-permute-start(f32[296,128]{1,0:T(8,128)S(1)} %collective-permute-done.24.refs_7_), channel_id=1, source_target_pairs={{0,4},{4,0},{1,5},{5,1},{2,6},{6,2},{3,7},{7,3},{8,12},{12,8},{9,1... | collective-permute-start | bytes 454664 | tf_op jit(solution)/shard_map/ppermute | solution.py:212
  41.9 1.9 %collective-permute-start.31 = (f32[296,128]{1,0:T(8,128)S(1)}, f32[296,128]{1,0:T(8,128)S(1)}, u32[]{:S(2)}, u32[]{:S(2)}) collective-permute-start(f32[296,128]{1,0:T(8,128)S(1)} %collective-permute-done.30.refs_9_), channel_id=1, source_target_pairs={{0,4},{4,0},{1,5},{5,1},{2,6},{6,2},{3,7},{7,3},{8,12},{12,8},{9,1... | collective-permute-start | bytes 454664 | tf_op jit(solution)/shard_map/ppermute | solution.py:212
  41.9 1.8 %collective-permute-start.27 = (f32[296,128]{1,0:T(8,128)S(1)}, f32[296,128]{1,0:T(8,128)S(1)}, u32[]{:S(2)}, u32[]{:S(2)}) collective-permute-start(f32[296,128]{1,0:T(8,128)S(1)} %collective-permute-done.26.refs_8_), channel_id=1, source_target_pairs={{0,4},{4,0},{1,5},{5,1},{2,6},{6,2},{3,7},{7,3},{8,12},{12,8},{9,1... | collective-permute-start | bytes 454664 | tf_op jit(solution)/shard_map/ppermute | solution.py:212
  45.7 13.3 %all-to-all-start.1 = ((f32[16,40,128]{2,1,0:T(8,128)}), f32[16,40,128]{2,1,0:T(8,128)S(1)}, u32[]{:S(2)}, u32[]{:S(2)}) async-start(f32[16,40,128]{2,1,0:T(8,128)} %product.2), calls=%async_computation.1 | async-start | bytes 655360 | tf_op jit(solution)/shard_map/all_to_all | solution.py:283
  60.0 0.6 %copy-start.3 = (f32[64,384]{1,0:T(8,128)}, f32[64,384]{1,0:T(8,128)S(1)}, u32[]{:S(2)}) copy-start(f32[64,384]{1,0:T(8,128)S(1)} %get-tuple-element.288) | copy-start | bytes 294916
